TPU v7x, 128 devices: a whole 4x4x4 slice. The times are simulated.
128 devices in a mesh: grp: 4 (over x), dap: 32 (over y, z, core).
Axes of the slice: x: 4, y: 4, z: 4, core: 2. Of those that a mesh axis runs over, the one named last changes fastest.
Arguments:
- pair_state: bfloat16 [8, 512, 512, 128], P('grp', 'dap'), may hold values from -6 to 6
- lengths: int32 [8], replicated, may hold values from 128 to 512, as said below
- norm_gain: float32 [3, 128], replicated, may hold values from 0.1 to 1.9
- norm_shift: float32 [3, 128], replicated, may hold values from -3 to 3
- attn_proj: bfloat16 [2, 128, 512], replicated
- bias_proj: bfloat16 [2, 128, 4], replicated, may hold values from -1.5 to 1.5
- attn_out: bfloat16 [2, 128, 128], replicated, may hold values from -0.5 to 0.5
- trans_up: bfloat16 [128, 512], replicated, may hold values from -0.5 to 0.5
- trans_down: bfloat16 [512, 128], replicated, may hold values from -0.25 to 0.25
Outputs:
- pair_out: bfloat16 [8, 512, 512, 128], P('grp', 'dap')
Inputs may be any that keep to these rules, and one draw needn't show every extreme that they name: `lengths`: residues of each protein; one protein has exactly 512.
All inputs are finite; a program needn't handle non-finite values.
Results may differ from a plain program's by a relative error of at most 0.035.
Values may be sent and summed in bfloat16 or wider, within the bound.
No kernel may reach another device: no remote copies, remote signals or barrier semaphores. Data moves between devices by JAX's collectives and lax.ppermute only.
A program may use at most 128 MiB of HBM per device.

v0:
```python
from functools import partial

import jax
import jax.numpy as jnp
from jax import lax
from jax.sharding import PartitionSpec as P

HEADS = 4
HEAD_DIM = 32
KEY_BLOCK = 128
ROW_BLOCK = 4


EPSILON = 1e-05
MASKED = -1000000000.0


def layer_norm(values, gain_row, shift_row):
    values = values.astype(jnp.float32)
    center = values - jnp.mean(values, -1, keepdims=True)
    spread = jnp.mean(center * center, -1, keepdims=True)
    return (center * lax.rsqrt(spread + EPSILON) * gain_row + shift_row).astype(jnp.bfloat16)


def lookup(table, index):
    return jnp.sum(jnp.where(jnp.arange(table.shape[0], dtype=jnp.int32) == index, table, 0))


def attention_block(projected, bias_one, length):
    row_count, width_all, four_chans = projected.shape
    chans = four_chans // 4
    query = (
        (projected[..., :chans] * HEAD_DIM ** (-0.5))
        .astype(jnp.bfloat16)
        .reshape(row_count, width_all, HEADS, HEAD_DIM)
    )
    keyed = (
        projected[..., chans : 2 * chans]
        .astype(jnp.bfloat16)
        .reshape(row_count, width_all, HEADS, HEAD_DIM)
    )
    valued = (
        projected[..., 2 * chans : 3 * chans]
        .astype(jnp.bfloat16)
        .reshape(row_count, width_all, HEADS, HEAD_DIM)
    )
    key_blocks = (length + KEY_BLOCK - 1) // KEY_BLOCK

    def one_step(block_index, carry):
        running_top, running_total, accum = carry
        key_start = block_index * KEY_BLOCK
        key_part = lax.dynamic_slice_in_dim(keyed, key_start, KEY_BLOCK, 1)
        value_part = lax.dynamic_slice_in_dim(valued, key_start, KEY_BLOCK, 1)
        bias_part = lax.dynamic_slice_in_dim(bias_one, key_start, KEY_BLOCK, 2)
        scores = jnp.einsum("rjhd,rkhd->rhjk", query, key_part, preferred_element_type=jnp.float32)
        scores = scores + bias_part.astype(jnp.float32)[None]
        live = key_start + jnp.arange(KEY_BLOCK, dtype=jnp.int32) < length
        scores = jnp.where(live, scores, MASKED)
        new_top = jnp.maximum(running_top, jnp.max(scores, -1))
        fading = jnp.exp(running_top - new_top)
        weights = jnp.exp(scores - new_top[..., None])
        running_total = running_total * fading + jnp.sum(weights, -1)
        accum = accum * fading[..., None] + jnp.einsum(
            "rhjk,rkhd->rhjd",
            weights.astype(jnp.bfloat16),
            value_part,
            preferred_element_type=jnp.float32,
        )
        return (new_top, running_total, accum)

    start_top = jnp.full((row_count, HEADS, width_all), -jnp.inf, jnp.float32)
    start_total = jnp.zeros((row_count, HEADS, width_all), jnp.float32)
    start_accum = jnp.zeros((row_count, HEADS, width_all, HEAD_DIM), jnp.float32)
    final_top, final_total, final_accum = lax.fori_loop(
        0, key_blocks, one_step, (start_top, start_total, start_accum)
    )
    mixed = final_accum / final_total[..., None]
    mixed = jnp.transpose(mixed, (0, 2, 1, 3)).reshape(row_count, width_all, chans)
    return (mixed * jax.nn.sigmoid(projected[..., 3 * chans :])).astype(jnp.bfloat16)


def row_update(normed_one, bias_one, length, proj_in, proj_out, offset):
    width_all = normed_one.shape[1]
    chans = normed_one.shape[2]
    rows_in = lax.dynamic_slice_in_dim(normed_one, offset, ROW_BLOCK, 0)
    projected = jnp.dot(rows_in.reshape(-1, chans), proj_in, preferred_element_type=jnp.float32)
    gated = attention_block(projected.reshape(ROW_BLOCK, width_all, 4 * chans), bias_one, length)
    result = jnp.dot(gated.reshape(-1, chans), proj_out, preferred_element_type=jnp.float32)
    return result.reshape(ROW_BLOCK, width_all, chans)


def trans_update(normed_one, up_proj, down_proj, offset):
    width_all = normed_one.shape[1]
    chans = normed_one.shape[2]
    rows_in = lax.dynamic_slice_in_dim(normed_one, offset, ROW_BLOCK, 0)
    hidden_units = jax.nn.relu(
        jnp.dot(rows_in.reshape(-1, chans), up_proj, preferred_element_type=jnp.float32)
    ).astype(jnp.bfloat16)
    result = jnp.dot(hidden_units, down_proj, preferred_element_type=jnp.float32)
    return result.reshape(ROW_BLOCK, width_all, chans)


def masked_blocks(compute, length, first_row, rows_dev, width_all, chans):
    col_live = jnp.arange(width_all, dtype=jnp.int32) < length

    def one_block(start):

        def work(offset):
            row_live = first_row + offset + jnp.arange(ROW_BLOCK, dtype=jnp.int32) < length
            cells = row_live[:, None, None] & col_live[None, :, None]
            return jnp.where(cells, compute(offset), 0.0)

        def skipped(offset):
            return jnp.zeros((ROW_BLOCK, width_all, chans), jnp.float32)

        return lax.cond(first_row + start < length, work, skipped, start)

    starts = jnp.arange(0, rows_dev, ROW_BLOCK, dtype=jnp.int32)
    return lax.map(one_block, starts).reshape(rows_dev, width_all, chans)


def attend(state, lens, first_row, gain_row, shift_row, proj_in, proj_bias, proj_out):
    per_group, rows_dev, width_all, chans = state.shape
    normed = layer_norm(state, gain_row, shift_row)
    bias_local = jnp.einsum(
        "prlc,ch->phrl", normed, proj_bias, preferred_element_type=jnp.float32
    ).astype(jnp.bfloat16)
    bias_all = lax.all_gather(bias_local, "dap", axis=2, tiled=True)
    updates = []
    for member in range(per_group):
        compute = partial(
            row_update, normed[member], bias_all[member], lens[member], proj_in, proj_out
        )
        updates.append(masked_blocks(compute, lens[member], first_row, rows_dev, width_all, chans))
    return (state.astype(jnp.float32) + jnp.stack(updates)).astype(jnp.bfloat16)


def transition(state, lens, first_row, gain_row, shift_row, up_proj, down_proj):
    per_group, rows_dev, width_all, chans = state.shape
    normed = layer_norm(state, gain_row, shift_row)
    updates = []
    for member in range(per_group):
        compute = partial(trans_update, normed[member], up_proj, down_proj)
        updates.append(masked_blocks(compute, lens[member], first_row, rows_dev, width_all, chans))
    return (state.astype(jnp.float32) + jnp.stack(updates)).astype(jnp.bfloat16)


def transpose_pair(state):
    arrived = lax.all_to_all(state, "dap", split_axis=2, concat_axis=1, tiled=True)
    return jnp.swapaxes(arrived, 1, 2)


def run_block(
    hosted, lens, norm_gain, norm_shift, attn_proj, bias_proj, attn_out, trans_up, trans_down
):
    first_row = lax.axis_index("dap") * hosted.shape[1]
    first = attend(
        hosted,
        lens,
        first_row,
        norm_gain[0],
        norm_shift[0],
        attn_proj[0],
        bias_proj[0],
        attn_out[0],
    )
    flipped = transpose_pair(first)
    second = attend(
        flipped,
        lens,
        first_row,
        norm_gain[1],
        norm_shift[1],
        attn_proj[1],
        bias_proj[1],
        attn_out[1],
    )
    third = transition(second, lens, first_row, norm_gain[2], norm_shift[2], trans_up, trans_down)
    return transpose_pair(third)


def on_device(
    pair_state, lengths, norm_gain, norm_shift, attn_proj, bias_proj, attn_out, trans_up, trans_down
):
    groups = lax.axis_size("grp")
    group = lax.axis_index("grp")
    per_group = pair_state.shape[0]
    table = lengths.reshape(groups, per_group)
    own_lens = lax.dynamic_index_in_dim(table, group, 0, keepdims=False)
    weights_all = (norm_gain, norm_shift, attn_proj, bias_proj, attn_out, trans_up, trans_down)
    group_ids = jnp.arange(groups, dtype=jnp.int32)
    order_first = jnp.argsort(-table[:, 0], stable=True)
    order_last = jnp.argsort(table[:, per_group - 1], stable=True)
    dest_of = jnp.sum(
        jnp.where(order_last[None, :] == group_ids[:, None], order_first[None, :], 0), 1
    )
    source_of = jnp.sum(
        jnp.where(order_first[None, :] == group_ids[:, None], order_last[None, :], 0), 1
    )
    mine_dest = lookup(dest_of, group)
    mine_source = lookup(source_of, group)
    guest_len = lookup(lengths, mine_source * per_group + per_group - 1)
    blank = jnp.zeros((groups,) + pair_state.shape[1:], jnp.bfloat16)
    outgoing = lax.dynamic_update_index_in_dim(blank, pair_state[per_group - 1], mine_dest, 0)
    arrived = lax.all_to_all(outgoing, "grp", split_axis=0, concat_axis=0, tiled=True)
    guest = lax.dynamic_index_in_dim(arrived, mine_source, 0, keepdims=True)
    hosted = jnp.concatenate([pair_state[: per_group - 1], guest], 0)
    hosted_lens = jnp.concatenate([own_lens[: per_group - 1], guest_len[None]], 0)
    result = run_block(hosted, hosted_lens, *weights_all)
    homeward = lax.dynamic_update_index_in_dim(blank, result[per_group - 1], mine_source, 0)
    returned = lax.all_to_all(homeward, "grp", split_axis=0, concat_axis=0, tiled=True)
    own_last = lax.dynamic_index_in_dim(returned, mine_dest, 0, keepdims=True)
    return jnp.concatenate([result[: per_group - 1], own_last], 0)


def solution(mesh):
    in_specs = (P("grp", "dap", None, None), P(), P(), P(), P(), P(), P(), P(), P())
    out_specs = P("grp", "dap", None, None)
    return jax.shard_map(
        on_device, mesh=mesh, in_specs=in_specs, out_specs=out_specs, check_vma=False
    )
```

profile of v0, /device:TPU:6, one launch (start us, length us, event | category | flops | bytes accessed | tf_op | source)
XLA Modules:
  0.0 1193.9 jit_solution(18386798959858692780)
XLA Ops:
  22.8 6.0 all-to-all-start
  35.2 85.6 %all-to-all-done = bf16[4,16,512,128]{3,1,2,0:T(8,128)(2,1)} async-done(((bf16[4,16,512,128]{3,1,2,0:T(8,128)(2,1)}), bf16[4,16,512,128]{3,1,2,0:T(8,128)(2,1)}, u32[]{:S(2)}, u32[]{:S(2)}) %all-to-all-start) | async-done | bytes 8388640 | tf_op jit(solution)/shard_map/all_to_all | solution.py:205
  126.7 29.5 %fusion.136 = f32[2,16,512]{1,2,0:T(8,128)S(1)} fusion(f32[2,16,512]{1,2,0:T(8,128)S(1)} %copy.246, bf16[1,16,512,128]{3,1,2,0:T(8,128)(2,1)} %copy-done.5, bf16[1,16,512,128]{3,1,2,0:T(8,128)(2,1)S(1)} %copy.304), kind=kLoop, calls=%fused_computation.194 | loop fusion | flops 10469376 | bytes 4325376 | tf_op jit(solution)/shard_map/reduce_sum | solution.py:21
  156.6 7.0 fusion.139
  165.6 9.8 fusion.148
  186.3 39.3 %all-gather.3.cloned.1.call-done = bf16[2,4,512,512]{3,1,0,2:T(4,128)(2,1)} async-done(((bf16[2,4,16,512]{3,1,0,2:T(4,128)(2,1)}), bf16[2,4,512,512]{3,1,0,2:T(4,128)(2,1)}) %all-gather.3.cloned.1.call-update) | async-done | bytes 4194320 | tf_op jit(solution)/shard_map/all_gather | solution.py:128
  235.3 122.7 %while.130 = (s32[]{:T(128)}, f32[4,4,512,128]{3,1,0,2:T(4,128)}, s32[4]{0:T(128)S(1)}, s32[]{:T(128)}, s32[]{:T(128)S(1)}, /*index=5*/bf16[16,512,128]{2,1,0:T(...) while((s32[]{:T(128)}, f32[4,4,512,128]{3,1,0,2:T(4,128)}, ...), condition=%wide.region_15.16_spmd.clone.clone, body=%wide.region_8.15_spmd.clone.clone.sunk | while | flops 485509888 | bytes 57683496 | solution.py:119
  236.7 27.6 %conditional.24 = (f32[1,4,512,128]{3,2,1,0:T(8,128)S(1)}) conditional(s32[]{:T(128)} %convert_element_type.267, () %tuple.342, (s32[]{:T(128)}, s32[]{:T(128)}, s32[]{:T(128)S(1)}, s32[512]{0:T(512)S(1)}, bf16[16,512,128]{2,1,0:T(8,128)(2,1)}, /*index=5*/bf16[128,512]{0,1:T(8,128)(2,1)S(1)}, bf16[4,512,512]{1,2,0:T(8,128)(2,1)}, ...), branch_computations={%region_9.9_spmd, %region_10.14_spmd} | conditional | flops 485509888 | bytes 55583572 | solution.py:116
  242.9 18.2 %while.126 = (s32[]{:T(128)}, f32[4,4,512]{2,1,0:T(4,128)S(1)}, f32[4,4,512]{2,1,0:T(4,128)S(1)}, f32[4,4,512,32]{2,3,1,0:T(8,128)S(1)}, s32[]{:T(128)}, /*index...) while((s32[]{:T(128)}, f32[4,4,512]{2,1,0:T(4,128)S(1)}, ...), condition=%wide.region_14.13_spmd, body=%wide.region_11.12_spmd.sunk | while | flops 146555136 | bytes 20710856 | solution.py:74
  267.4 27.6 %conditional.24 = (f32[1,4,512,128]{3,2,1,0:T(8,128)S(1)}) conditional(s32[]{:T(128)} %convert_element_type.267, () %tuple.342, (s32[]{:T(128)}, s32[]{:T(128)}, s32[]{:T(128)S(1)}, s32[512]{0:T(512)S(1)}, bf16[16,512,128]{2,1,0:T(8,128)(2,1)}, /*index=5*/bf16[128,512]{0,1:T(8,128)(2,1)S(1)}, bf16[4,512,512]{1,2,0:T(8,128)(2,1)}, ...), branch_computations={%region_9.9_spmd, %region_10.14_spmd} | conditional | flops 485509888 | bytes 55583572 | solution.py:116
  273.6 18.2 %while.126 = (s32[]{:T(128)}, f32[4,4,512]{2,1,0:T(4,128)S(1)}, f32[4,4,512]{2,1,0:T(4,128)S(1)}, f32[4,4,512,32]{2,3,1,0:T(8,128)S(1)}, s32[]{:T(128)}, /*index...) while((s32[]{:T(128)}, f32[4,4,512]{2,1,0:T(4,128)S(1)}, ...), condition=%wide.region_14.13_spmd, body=%wide.region_11.12_spmd.sunk | while | flops 146555136 | bytes 20710856 | solution.py:74
  298.1 27.6 %conditional.24 = (f32[1,4,512,128]{3,2,1,0:T(8,128)S(1)}) conditional(s32[]{:T(128)} %convert_element_type.267, () %tuple.342, (s32[]{:T(128)}, s32[]{:T(128)}, s32[]{:T(128)S(1)}, s32[512]{0:T(512)S(1)}, bf16[16,512,128]{2,1,0:T(8,128)(2,1)}, /*index=5*/bf16[128,512]{0,1:T(8,128)(2,1)S(1)}, bf16[4,512,512]{1,2,0:T(8,128)(2,1)}, ...), branch_computations={%region_9.9_spmd, %region_10.14_spmd} | conditional | flops 485509888 | bytes 55583572 | solution.py:116
  304.3 18.2 %while.126 = (s32[]{:T(128)}, f32[4,4,512]{2,1,0:T(4,128)S(1)}, f32[4,4,512]{2,1,0:T(4,128)S(1)}, f32[4,4,512,32]{2,3,1,0:T(8,128)S(1)}, s32[]{:T(128)}, /*index...) while((s32[]{:T(128)}, f32[4,4,512]{2,1,0:T(4,128)S(1)}, ...), condition=%wide.region_14.13_spmd, body=%wide.region_11.12_spmd.sunk | while | flops 146555136 | bytes 20710856 | solution.py:74
  328.8 27.6 %conditional.24 = (f32[1,4,512,128]{3,2,1,0:T(8,128)S(1)}) conditional(s32[]{:T(128)} %convert_element_type.267, () %tuple.342, (s32[]{:T(128)}, s32[]{:T(128)}, s32[]{:T(128)S(1)}, s32[512]{0:T(512)S(1)}, bf16[16,512,128]{2,1,0:T(8,128)(2,1)}, /*index=5*/bf16[128,512]{0,1:T(8,128)(2,1)S(1)}, bf16[4,512,512]{1,2,0:T(8,128)(2,1)}, ...), branch_computations={%region_9.9_spmd, %region_10.14_spmd} | conditional | flops 485509888 | bytes 55583572 | solution.py:116
  334.9 18.2 %while.126 = (s32[]{:T(128)}, f32[4,4,512]{2,1,0:T(4,128)S(1)}, f32[4,4,512]{2,1,0:T(4,128)S(1)}, f32[4,4,512,32]{2,3,1,0:T(8,128)S(1)}, s32[]{:T(128)}, /*index...) while((s32[]{:T(128)}, f32[4,4,512]{2,1,0:T(4,128)S(1)}, ...), condition=%wide.region_14.13_spmd, body=%wide.region_11.12_spmd.sunk | while | flops 146555136 | bytes 20710856 | solution.py:74
  364.8 100.3 %while.131 = (s32[]{:T(128)}, f32[4,4,512,128]{3,1,0,2:T(4,128)}, s32[4]{0:T(128)S(1)}, s32[]{:T(128)}, s32[]{:T(128)}, /*index=5*/bf16[16,512,128]{2,1,0:T(8,12...) while((s32[]{:T(128)}, f32[4,4,512,128]{3,1,0,2:T(4,128)}, ...), condition=%wide.region_24.25_spmd.clone.clone, body=%wide.region_17.24_spmd.clone.clone.sunk | while | flops 485509888 | bytes 57683496 | solution.py:119
  367.3 21.3 %conditional.25 = (f32[1,4,512,128]{3,2,1,0:T(8,128)S(1)}) conditional(s32[]{:T(128)} %convert_element_type.268, () %tuple.345, (s32[]{:T(128)}, s32[]{:T(128)}, s32[]{:T(128)}, s32[512]{0:T(512)S(1)}, bf16[16,512,128]{2,1,0:T(8,128)(2,1)}, /*index=5*/bf16[128,512]{0,1:T(8,128)(2,1)S(1)}, bf16[4,512,512]{1,2,0:T(8,128)(2,1)}, ...), branch_computations={%region_18.18_spmd, %region_19.23_spmd} | conditional | flops 485509888 | bytes 55583572 | solution.py:116
  374.0 10.3 while.127
  392.2 21.3 %conditional.25 = (f32[1,4,512,128]{3,2,1,0:T(8,128)S(1)}) conditional(s32[]{:T(128)} %convert_element_type.268, () %tuple.345, (s32[]{:T(128)}, s32[]{:T(128)}, s32[]{:T(128)}, s32[512]{0:T(512)S(1)}, bf16[16,512,128]{2,1,0:T(8,128)(2,1)}, /*index=5*/bf16[128,512]{0,1:T(8,128)(2,1)S(1)}, bf16[4,512,512]{1,2,0:T(8,128)(2,1)}, ...), branch_computations={%region_18.18_spmd, %region_19.23_spmd} | conditional | flops 485509888 | bytes 55583572 | solution.py:116
  398.9 10.3 while.127
  417.2 21.3 %conditional.25 = (f32[1,4,512,128]{3,2,1,0:T(8,128)S(1)}) conditional(s32[]{:T(128)} %convert_element_type.268, () %tuple.345, (s32[]{:T(128)}, s32[]{:T(128)}, s32[]{:T(128)}, s32[512]{0:T(512)S(1)}, bf16[16,512,128]{2,1,0:T(8,128)(2,1)}, /*index=5*/bf16[128,512]{0,1:T(8,128)(2,1)S(1)}, bf16[4,512,512]{1,2,0:T(8,128)(2,1)}, ...), branch_computations={%region_18.18_spmd, %region_19.23_spmd} | conditional | flops 485509888 | bytes 55583572 | solution.py:116
  423.9 10.3 while.127
  442.2 21.3 %conditional.25 = (f32[1,4,512,128]{3,2,1,0:T(8,128)S(1)}) conditional(s32[]{:T(128)} %convert_element_type.268, () %tuple.345, (s32[]{:T(128)}, s32[]{:T(128)}, s32[]{:T(128)}, s32[512]{0:T(512)S(1)}, bf16[16,512,128]{2,1,0:T(8,128)(2,1)}, /*index=5*/bf16[128,512]{0,1:T(8,128)(2,1)S(1)}, bf16[4,512,512]{1,2,0:T(8,128)(2,1)}, ...), branch_computations={%region_18.18_spmd, %region_19.23_spmd} | conditional | flops 485509888 | bytes 55583572 | solution.py:116
  448.9 10.3 while.127
  470.9 54.6 %all_to_all.39 = bf16[2,16,512,128]{3,1,0,2:T(8,128)(2,1)S(1)} all-to-all(bf16[2,16,512,128]{3,1,0,2:T(8,128)(2,1)S(1)} %copy.257), channel_id=1, replica_groups=mesh['grp'=4,'dap'=32] {'dap'}, dimensions={2} | all-to-all | bytes 8388608 | tf_op jit(solution)/shard_map/all_to_all | solution.py:149
  526.7 10.8 copy.258
  537.5 5.9 reduce_sum.142
  543.9 7.5 multiply_reduce_fusion
  551.9 7.6 add_convert_fusion
  561.6 9.8 fusion.149
  579.5 58.0 %all-gather.5.cloned.1.call-done = bf16[2,4,512,512]{3,1,0,2:T(4,128)(2,1)} async-done(((bf16[2,4,16,512]{3,1,0,2:T(4,128)(2,1)}), bf16[2,4,512,512]{3,1,0,2:T(4,128)(2,1)}) %all-gather.5.cloned.1.call-update) | async-done | bytes 4194320 | tf_op jit(solution)/shard_map/all_gather | solution.py:128
  647.1 121.5 %while.132 = (s32[]{:T(128)}, f32[4,4,512,128]{3,1,0,2:T(4,128)}, s32[4]{0:T(128)S(1)}, s32[]{:T(128)}, s32[]{:T(128)S(1)}, /*index=5*/bf16[16,512,128]{2,1,0:T(...) while((s32[]{:T(128)}, f32[4,4,512,128]{3,1,0,2:T(4,128)}, ...), condition=%wide.region_34.35_spmd.clone.clone, body=%wide.region_27.34_spmd.clone.clone.sunk | while | flops 485509888 | bytes 57683496 | solution.py:119
  648.4 27.3 %conditional.26 = (f32[1,4,512,128]{3,2,1,0:T(8,128)S(1)}) conditional(s32[]{:T(128)} %convert_element_type.269, () %tuple.348, (s32[]{:T(128)}, s32[]{:T(128)}, s32[]{:T(128)S(1)}, s32[512]{0:T(512)S(1)}, bf16[16,512,128]{2,1,0:T(8,128)(2,1)}, /*index=5*/bf16[128,512]{0,1:T(8,128)(2,1)S(1)}, bf16[4,512,512]{1,2,0:T(8,128)(2,1)}, ...), branch_computations={%region_28.28_spmd, %region_29.33_spmd} | conditional | flops 485509888 | bytes 55583572 | solution.py:116
  654.4 18.2 %while.128 = (s32[]{:T(128)}, f32[4,4,512]{2,1,0:T(4,128)S(1)}, f32[4,4,512]{2,1,0:T(4,128)S(1)}, f32[4,4,512,32]{2,3,1,0:T(8,128)S(1)}, s32[]{:T(128)}, /*index...) while((s32[]{:T(128)}, f32[4,4,512]{2,1,0:T(4,128)S(1)}, ...), condition=%wide.region_33.32_spmd, body=%wide.region_30.31_spmd.sunk | while | flops 146555136 | bytes 20710856 | solution.py:74
  678.8 27.3 %conditional.26 = (f32[1,4,512,128]{3,2,1,0:T(8,128)S(1)}) conditional(s32[]{:T(128)} %convert_element_type.269, () %tuple.348, (s32[]{:T(128)}, s32[]{:T(128)}, s32[]{:T(128)S(1)}, s32[512]{0:T(512)S(1)}, bf16[16,512,128]{2,1,0:T(8,128)(2,1)}, /*index=5*/bf16[128,512]{0,1:T(8,128)(2,1)S(1)}, bf16[4,512,512]{1,2,0:T(8,128)(2,1)}, ...), branch_computations={%region_28.28_spmd, %region_29.33_spmd} | conditional | flops 485509888 | bytes 55583572 | solution.py:116
  684.8 18.2 %while.128 = (s32[]{:T(128)}, f32[4,4,512]{2,1,0:T(4,128)S(1)}, f32[4,4,512]{2,1,0:T(4,128)S(1)}, f32[4,4,512,32]{2,3,1,0:T(8,128)S(1)}, s32[]{:T(128)}, /*index...) while((s32[]{:T(128)}, f32[4,4,512]{2,1,0:T(4,128)S(1)}, ...), condition=%wide.region_33.32_spmd, body=%wide.region_30.31_spmd.sunk | while | flops 146555136 | bytes 20710856 | solution.py:74
  709.2 27.3 %conditional.26 = (f32[1,4,512,128]{3,2,1,0:T(8,128)S(1)}) conditional(s32[]{:T(128)} %convert_element_type.269, () %tuple.348, (s32[]{:T(128)}, s32[]{:T(128)}, s32[]{:T(128)S(1)}, s32[512]{0:T(512)S(1)}, bf16[16,512,128]{2,1,0:T(8,128)(2,1)}, /*index=5*/bf16[128,512]{0,1:T(8,128)(2,1)S(1)}, bf16[4,512,512]{1,2,0:T(8,128)(2,1)}, ...), branch_computations={%region_28.28_spmd, %region_29.33_spmd} | conditional | flops 485509888 | bytes 55583572 | solution.py:116
  715.2 18.2 %while.128 = (s32[]{:T(128)}, f32[4,4,512]{2,1,0:T(4,128)S(1)}, f32[4,4,512]{2,1,0:T(4,128)S(1)}, f32[4,4,512,32]{2,3,1,0:T(8,128)S(1)}, s32[]{:T(128)}, /*index...) while((s32[]{:T(128)}, f32[4,4,512]{2,1,0:T(4,128)S(1)}, ...), condition=%wide.region_33.32_spmd, body=%wide.region_30.31_spmd.sunk | while | flops 146555136 | bytes 20710856 | solution.py:74
  739.6 27.3 %conditional.26 = (f32[1,4,512,128]{3,2,1,0:T(8,128)S(1)}) conditional(s32[]{:T(128)} %convert_element_type.269, () %tuple.348, (s32[]{:T(128)}, s32[]{:T(128)}, s32[]{:T(128)S(1)}, s32[512]{0:T(512)S(1)}, bf16[16,512,128]{2,1,0:T(8,128)(2,1)}, /*index=5*/bf16[128,512]{0,1:T(8,128)(2,1)S(1)}, bf16[4,512,512]{1,2,0:T(8,128)(2,1)}, ...), branch_computations={%region_28.28_spmd, %region_29.33_spmd} | conditional | flops 485509888 | bytes 55583572 | solution.py:116
  745.6 18.2 %while.128 = (s32[]{:T(128)}, f32[4,4,512]{2,1,0:T(4,128)S(1)}, f32[4,4,512]{2,1,0:T(4,128)S(1)}, f32[4,4,512,32]{2,3,1,0:T(8,128)S(1)}, s32[]{:T(128)}, /*index...) while((s32[]{:T(128)}, f32[4,4,512]{2,1,0:T(4,128)S(1)}, ...), condition=%wide.region_33.32_spmd, body=%wide.region_30.31_spmd.sunk | while | flops 146555136 | bytes 20710856 | solution.py:74
  775.4 99.4 %while.133 = (s32[]{:T(128)}, f32[4,4,512,128]{3,1,0,2:T(4,128)}, s32[4]{0:T(128)S(1)}, s32[]{:T(128)}, s32[]{:T(128)}, /*index=5*/bf16[16,512,128]{2,1,0:T(8,12...) while((s32[]{:T(128)}, f32[4,4,512,128]{3,1,0,2:T(4,128)}, ...), condition=%wide.region_42.43_spmd.clone.clone, body=%wide.region_35.42_spmd.clone.clone.sunk | while | flops 485509888 | bytes 57683496 | solution.py:119
  777.5 21.2 %conditional.27 = (f32[1,4,512,128]{3,2,1,0:T(8,128)S(1)}) conditional(s32[]{:T(128)} %convert_element_type.270, () %tuple.351, (s32[]{:T(128)}, s32[]{:T(128)}, s32[]{:T(128)}, s32[512]{0:T(512)S(1)}, bf16[16,512,128]{2,1,0:T(8,128)(2,1)}, /*index=5*/bf16[128,512]{0,1:T(8,128)(2,1)S(1)}, bf16[4,512,512]{1,2,0:T(8,128)(2,1)}, ...), branch_computations={%region_36.36_spmd, %region_37.41_spmd} | conditional | flops 485509888 | bytes 55583572 | solution.py:116
  784.1 10.3 while.129
  802.3 21.2 %conditional.27 = (f32[1,4,512,128]{3,2,1,0:T(8,128)S(1)}) conditional(s32[]{:T(128)} %convert_element_type.270, () %tuple.351, (s32[]{:T(128)}, s32[]{:T(128)}, s32[]{:T(128)}, s32[512]{0:T(512)S(1)}, bf16[16,512,128]{2,1,0:T(8,128)(2,1)}, /*index=5*/bf16[128,512]{0,1:T(8,128)(2,1)S(1)}, bf16[4,512,512]{1,2,0:T(8,128)(2,1)}, ...), branch_computations={%region_36.36_spmd, %region_37.41_spmd} | conditional | flops 485509888 | bytes 55583572 | solution.py:116
  808.9 10.3 while.129
  827.2 21.2 %conditional.27 = (f32[1,4,512,128]{3,2,1,0:T(8,128)S(1)}) conditional(s32[]{:T(128)} %convert_element_type.270, () %tuple.351, (s32[]{:T(128)}, s32[]{:T(128)}, s32[]{:T(128)}, s32[512]{0:T(512)S(1)}, bf16[16,512,128]{2,1,0:T(8,128)(2,1)}, /*index=5*/bf16[128,512]{0,1:T(8,128)(2,1)S(1)}, bf16[4,512,512]{1,2,0:T(8,128)(2,1)}, ...), branch_computations={%region_36.36_spmd, %region_37.41_spmd} | conditional | flops 485509888 | bytes 55583572 | solution.py:116
  833.7 10.3 while.129
  852.0 21.2 %conditional.27 = (f32[1,4,512,128]{3,2,1,0:T(8,128)S(1)}) conditional(s32[]{:T(128)} %convert_element_type.270, () %tuple.351, (s32[]{:T(128)}, s32[]{:T(128)}, s32[]{:T(128)}, s32[512]{0:T(512)S(1)}, bf16[16,512,128]{2,1,0:T(8,128)(2,1)}, /*index=5*/bf16[128,512]{0,1:T(8,128)(2,1)S(1)}, bf16[4,512,512]{1,2,0:T(8,128)(2,1)}, ...), branch_computations={%region_36.36_spmd, %region_37.41_spmd} | conditional | flops 485509888 | bytes 55583572 | solution.py:116
  858.6 10.3 while.129
  874.9 6.6 fusion.142
  887.1 14.6 %fusion.132 = f32[2,16,512]{1,0,2:T(2,128)S(1)} fusion(bf16[2,16,512,128]{3,1,0,2:T(8,128)(2,1)} %copy-done.7, f32[2,16,512]{1,0,2:T(2,128)S(1)} %copy.273), kind=kLoop, calls=%fused_computation.190 | loop fusion | flops 8372224 | bytes 4325376 | tf_op jit(solution)/shard_map/reduce_sum | solution.py:21
  902.2 8.2 fusion.135
  916.8 33.6 %while.134 = (s32[]{:T(128)}, f32[4,4,512,128]{3,1,0,2:T(4,128)}, s32[4]{0:T(128)S(1)}, s32[]{:T(128)}, s32[]{:T(128)S(1)}, /*index=5*/bf16[16,512,128]{2,1,0:T(...) while((s32[]{:T(128)}, f32[4,4,512,128]{3,1,0,2:T(4,128)}, ...), condition=%wide.region_48.49_spmd.clone.clone, body=%wide.region_45.48_spmd.clone.clone.sunk | while | flops 539232768 | bytes 7087889 | solution.py:119
  918.1 5.3 conditional.28
  926.5 5.3 conditional.28
  943.3 5.3 conditional.28
  956.4 40.4 %while.135 = (s32[]{:T(128)}, f32[4,4,512,128]{3,1,0,2:T(4,128)}, s32[4]{0:T(128)S(1)}, s32[]{:T(128)}, s32[]{:T(128)}, /*index=5*/bf16[16,512,128]{2,1,0:T(8,12...) while((s32[]{:T(128)}, f32[4,4,512,128]{3,1,0,2:T(4,128)}, ...), condition=%wide.region_52.53_spmd.clone.clone, body=%wide.region_49.52_spmd.clone.clone.sunk | while | flops 539232768 | bytes 7087889 | solution.py:119
  958.3 6.5 conditional.29
  968.4 6.5 conditional.29
  978.5 6.5 conditional.29
  988.6 6.5 conditional.29
  996.8 9.3 fusion.141
  1006.1 54.7 %all_to_all.37 = bf16[2,16,512,128]{3,1,0,2:T(8,128)(2,1)S(1)} all-to-all(bf16[2,16,512,128]{3,1,0,2:T(8,128)(2,1)S(1)} %fusion.141), channel_id=1, replica_groups=mesh['grp'=4,'dap'=32] {'dap'}, dimensions={2} | all-to-all | bytes 8388608 | tf_op jit(solution)/shard_map/all_to_all | solution.py:149
  1065.5 117.3 %all_to_all.38 = bf16[4,16,512,128]{3,1,2,0:T(8,128)(2,1)S(1)} all-to-all(bf16[4,16,512,128]{3,1,2,0:T(8,128)(2,1)S(1)} %get-tuple-element.1636), channel_id=1, replica_groups=mesh['grp'=4,'dap'=32] {'grp'}, dimensions={0} | all-to-all | bytes 16777216 | tf_op jit(solution)/shard_map/all_to_all | solution.py:211
  (853 shorter events, 540.7 us)
Async XLA Ops:
  22.8 97.9 %all-to-all-start = ((bf16[4,16,512,128]{3,1,2,0:T(8,128)(2,1)}), bf16[4,16,512,128]{3,1,2,0:T(8,128)(2,1)}, u32[]{:S(2)}, u32[]{:S(2)}) async-start(bf16[4,16,512,128]{3,1,2,0:T(8,128)(2,1)} %copy_dynamic-update-slice_fusion.6), calls=%async_computation | async-start | bytes 16777216 | tf_op jit(solution)/shard_map/all_to_all | solution.py:205
  28.8 5.8 copy-start.20
  28.8 5.8 copy-start.21
  28.8 196.7 %all-gather.3.cloned.1.call-start = ((), (), s32[]{:S(2)}) async-start(), calls=%async_computation.4 | async-start | bytes 4325376 | tf_op jit(solution)/shard_map/all_gather | solution.py:128
  33.9 122.7 %copy-start.4 = (bf16[1,16,512,128]{3,1,2,0:T(8,128)(2,1)}, bf16[1,16,512,128]{3,1,2,0:T(8,128)(2,1)S(1)}, u32[]{:S(2)}) copy-start(bf16[1,16,512,128]{3,1,2,0:T(8,128)(2,1)S(1)} %copy.304) | copy-start | bytes 6291460
  122.7 1.4 copy-start.5
  156.5 9.0 copy-start.23
  163.5 2.0 copy-start.6
  165.5 11.2 copy-start.11
  165.5 12.7 %copy-start.22 = (s32[8]{0:T(128)S(1)}, s32[8]{0:T(128)}, u32[]{:S(2)}) copy-start(s32[8]{0:T(128)} %param.42) | copy-start | bytes 100
  165.5 13.4 %copy-start.15 = (bf16[2,128,128]{2,1,0:T(8,128)(2,1)S(1)}, bf16[2,128,128]{2,1,0:T(8,128)(2,1)}, u32[]{:S(2)}) copy-start(bf16[2,128,128]{2,1,0:T(8,128)(2,1)} %param.47) | copy-start | bytes 196612
  176.7 460.9 %all-gather.5.cloned.1.call-start = ((), (), s32[]{:S(2)}) async-start(), calls=%async_computation.5 | async-start | bytes 4325376 | tf_op jit(solution)/shard_map/all_gather | solution.py:128
  240.6 2.0 copy-start
  271.3 2.0 copy-start
  302.0 2.0 copy-start
  332.6 2.0 copy-start
  358.0 6.8 copy-start.12
  371.7 1.9 copy-start.1
  396.7 1.9 copy-start.1
  421.7 1.9 copy-start.1
  446.6 1.9 copy-start.1
  543.9 8.0 copy-start.18
  543.9 8.0 copy-start.19
  551.9 9.7 copy-start.24
  559.6 2.0 copy-start.8
  561.6 11.1 copy-start.10
  641.6 5.5 copy-start.9
  641.6 5.5 copy-start.13
  652.1 2.0 copy-start.2
  682.5 2.0 copy-start.2
  712.9 2.0 copy-start.2
  743.3 2.0 copy-start.2
  781.8 2.0 copy-start.3
  806.6 2.0 copy-start.3
  831.4 2.0 copy-start.3
  856.3 2.0 copy-start.3
  881.5 2.0 copy-start.7
  886.6 15.5 %copy-start.16 = (f32[128]{0:T(128)S(1)}, f32[128]{0:T(128)}, u32[]{:S(2)}) copy-start(f32[128]{0:T(128)} %get-tuple-element.1656) | copy-start | bytes 1540
  886.7 15.5 %copy-start.17 = (f32[128]{0:T(128)S(1)}, f32[128]{0:T(128)}, u32[]{:S(2)}) copy-start(f32[128]{0:T(128)} %get-tuple-element.1661) | copy-start | bytes 1540
  912.4 4.4 copy-start.14
  912.4 4.4 copy-start.25
  912.4 4.4 copy-start.26
Sparse Core Ops, SparseCore 0:
  176.8 48.6 all-gather.2
  572.8 64.6 all-gather.4
where the time goes:
time: 1210 us; the launch traced here: 1190 us
  other arithmetic  278 us (23%)
  blocking collectives  227 us (19%)
  local copies, waits for them, and re-layouts  208 us (17%)
  waiting for transfers between devices  183 us (15%)
  matrix products  175 us (14%)
  loops' own time  97.1 us (8%)
  between operations  19.2 us (2%)
    all_to_all x1, blocking collectives, on_device(): lax.all_to_all(homeward, 'grp', split_axis=0, concat_axis=0, tiled=True)  117 us
    all_to_all x2, blocking collectives, transpose_pair(): lax.all_to_all(state, 'dap', split_axis=2, concat_axis=1, tiled=True)  109 us
    all_gather x2, waiting for transfers between devices, attend(): bias_all = lax.all_gather(bias_local, 'dap', axis=2, tiled=True)  97.3 us
    all_to_all x1, waiting for transfers between devices, on_device(): lax.all_to_all(outgoing, 'grp', split_axis=0, concat_axis=0, tiled=True)  85.6 us
    another operation x24, loops' own time, one_block(): return lax.cond(first_row + start < length, work, skipped, start)  69.2 us
    dot_general x48, matrix products, one_step(): jnp.einsum('rhjk,rkhd->rhjd', weights.astype(jnp.bfloat16), value_part, p...  57.9 us
    convert_element_type x48, other arithmetic, one_step(): scores = scores + bias_part.astype(jnp.float32)[None]  56.2 us
    reduce_sum x3, other arithmetic, layer_norm(): spread = jnp.mean(center * center, -1, keepdims=True)  51.6 us
  transfers between devices with their start and end apart: 3, of which 3 were waited for; matrix products, arithmetic and copies ran while one was open for 2% of the time, Pallas kernels for 0%

commit v1 on v0

v1 whole, which is shorter than its diff:
```python
from functools import partial

import jax
import jax.numpy as jnp
from jax import lax
from jax.experimental import pallas as pl
from jax.experimental.pallas import tpu as pltpu
from jax.sharding import PartitionSpec as P

HEADS = 4
HEAD_DIM = 32
CHANS = 128
RES = 512
DEVS = 32
ROWS = 16
HIDDEN = 512
EPSILON = 1e-05
LOG2E = 1.4426950408889634
MASKED = -1e30
SAFE_SQUARED = 90.0**2
WIDTHS = (256, 384, 512)
BF = jnp.bfloat16
F32 = jnp.float32
VMEM_LIMIT = 48 * 2**20


def layer_norm(values, gain_row, shift_row):
    center = values - jnp.mean(values, -1, keepdims=True)
    spread = jnp.mean(center * center, -1, keepdims=True)
    return (center * lax.rsqrt(spread + EPSILON) * gain_row + shift_row).astype(BF)


def dot_nn(left, right):
    return jnp.dot(left, right, preferred_element_type=F32)


def dot_nt(left, right):
    return lax.dot_general(left, right, (((1,), (1,)), ((), ())), preferred_element_type=F32)


def first_bias_kernel(x_ref, gain_ref, shift_ref, bpt_ref, out_ref, rows_scr):
    r = pl.program_id(1)
    y = layer_norm(x_ref[0, 0].astype(F32), gain_ref[...], shift_ref[...])
    b = dot_nt(bpt_ref[...], y)
    for h in range(HEADS):
        rows_scr[pl.ds(h * ROWS + r, 1), :] = b[h : h + 1]

    @pl.when(r == ROWS - 1)
    def _():
        out_ref[0] = rows_scr[...].astype(BF)


def first_bias(state, gain, shift, bpt):
    pairs = state.shape[0]
    whole = lambda a: pl.BlockSpec(a.shape, lambda p, r: (0,) * a.ndim)
    return pl.pallas_call(
        first_bias_kernel,
        grid=(pairs, ROWS),
        in_specs=[pl.BlockSpec((1, 1, RES, CHANS), lambda p, r: (p, r, 0, 0))]
        + [whole(a) for a in (gain, shift, bpt)],
        out_specs=pl.BlockSpec((1, HEADS * ROWS, RES), lambda p, r: (p, 0, 0)),
        out_shape=jax.ShapeDtypeStruct((pairs, HEADS * ROWS, RES), BF),
        scratch_shapes=[pltpu.VMEM((HEADS * ROWS, RES), F32)],
        name="first_bias",
    )(state, gain, shift, bpt)


def attend_kernel(
    flipped,
    info_ref,
    x_ref,
    bias_ref,
    gain_ref,
    shift_ref,
    gain2_ref,
    shift2_ref,
    w_ref,
    wkt_ref,
    wo_ref,
    extra_ref,
    down_ref,
    out_ref,
    bias_out_ref,
    biasf,
    vblk,
    qm,
    kts,
    gate,
    mixed,
    line,
    bias_rows,
):
    step = pl.program_id(0)
    n = info_ref[0]
    row = info_ref[1] + step * info_ref[2]
    head_of = lax.broadcasted_iota(jnp.int32, (1, CHANS), 1) // HEAD_DIM

    def load_x(width):
        if flipped:
            return x_ref[: width // ROWS, 0].reshape(width, CHANS).astype(F32)
        return x_ref[0, :width].astype(F32)

    def load_rest(width):
        if flipped:
            return x_ref[width // ROWS :, 0].reshape(RES - width, CHANS).astype(F32)
        return x_ref[0, width:].astype(F32)

    @pl.when(step == 0)
    def _():
        klive = lax.broadcasted_iota(jnp.int32, (1, RES), 1) < n
        for h in range(HEADS):
            b = bias_ref[:, 0, h * ROWS : (h + 1) * ROWS].reshape(RES, RES).astype(F32)
            if flipped:
                b = b.T
            b = jnp.where(klive, b * LOG2E, MASKED)
            biasf[h] = b - jnp.max(b, -1, keepdims=True)
            vblk[h, :, CHANS:] = jnp.broadcast_to(
                (head_of == h).astype(F32).astype(BF), (RES, CHANS)
            )

    def put(start, values):
        size = values.shape[0]
        line[pl.ds(start * ROWS + step, size, stride=ROWS), :] = values

    def work(width):
        x = load_x(width)
        y = layer_norm(x, gain_ref[...], shift_ref[...])
        proj = dot_nn(y, w_ref[...])
        q = proj[:, :CHANS] * (HEAD_DIM**-0.5 * LOG2E)
        v = proj[:, CHANS : 2 * CHANS]
        gate[:width] = jax.nn.sigmoid(proj[:, 2 * CHANS :])
        kt = dot_nt(wkt_ref[...], y)
        kts[:, :width] = kt.astype(BF)
        for h in range(HEADS):
            qm[h, :width] = jnp.where(head_of == h, q, 0.0).astype(BF)
            vblk[h, :width, :CHANS] = jnp.where(head_of == h, v, 0.0).astype(BF)
        same = (
            lax.broadcasted_iota(jnp.int32, (CHANS, CHANS), 0) // HEAD_DIM == head_of
        ).astype(F32).astype(BF)
        q_top = jnp.max(dot_nn((q * q).astype(BF), same))
        k_top = jnp.max(jnp.sum((kt * kt).reshape(HEADS, HEAD_DIM, width), 1))
        acc = jnp.zeros((width, 2 * CHANS), F32)
        for h in range(HEADS):
            s = dot_nn(qm[h, :width], kts[:, :width]) + biasf[h, :width, :width]
            acc += dot_nn(jnp.exp2(s).astype(BF), vblk[h, :width])
        mixed[:width] = acc[:, :CHANS] / acc[:, CHANS:]

        @pl.when(jnp.logical_not(q_top * k_top < SAFE_SQUARED))
        def _():
            def block(t, _):
                at = pl.ds(pl.multiple_of(t * 128, 128), 128)
                acc = jnp.zeros((128, 2 * CHANS), F32)
                for h in range(HEADS):
                    s = dot_nn(qm[h, at], kts[:, :width]) + biasf[h, at, :width]
                    s = s - jnp.max(s, -1, keepdims=True)
                    acc += dot_nn(jnp.exp2(s).astype(BF), vblk[h, :width])
                mixed[at] = acc[:, :CHANS] / acc[:, CHANS:]
                return 0

            lax.fori_loop(0, width // 128, block, 0)

        gated = (mixed[:width] * gate[:width]).astype(BF)
        live = lax.broadcasted_iota(jnp.int32, (width, 1), 0) < n
        update = jnp.where(live, dot_nn(gated, wo_ref[...]), 0.0)
        result = (load_x(width) + update).astype(BF).astype(F32)
        normed = layer_norm(result, gain2_ref[...], shift2_ref[...])
        if flipped:
            hidden = jax.nn.relu(dot_nn(normed, extra_ref[...])).astype(BF)
            update = jnp.where(live, dot_nn(hidden, down_ref[...]), 0.0)
            put(0, result + update)
        else:
            put(0, result)
            b = dot_nt(extra_ref[...], normed)
            for h in range(HEADS):
                bias_rows[pl.ds(h * ROWS + step, 1), :width] = b[h : h + 1]
        if width < RES:
            put(width, load_rest(width))

    low = 0
    for width in WIDTHS:

        @pl.when((row < n) & (n > low) & (n <= width))
        def _(width=width):
            work(width)

        low = width

    @pl.when(row >= n)
    def _():
        put(0, load_x(RES))

    @pl.when(step == ROWS - 1)
    def _():
        if flipped:
            for d in range(DEVS):
                out_ref[d] = (
                    line[d * ROWS * ROWS : (d + 1) * ROWS * ROWS].reshape(ROWS, ROWS, CHANS).astype(BF)
                )
            bias_out_ref[...] = jnp.zeros_like(bias_out_ref)
        else:
            for c in range(ROWS):
                out_ref[:, c] = (
                    line[c * RES : (c + 1) * RES].reshape(DEVS, ROWS, CHANS).astype(BF)
                )
            bias_out_ref[...] = bias_rows[...].astype(BF)


def attend(flipped, member, info, state, bias, gain, shift, gain2, shift2, w, wkt, wo, extra, down):
    whole = lambda a: pl.BlockSpec(a.shape, lambda i, s: (0,) * a.ndim)
    if flipped:
        x_spec = pl.BlockSpec((DEVS, 1, ROWS, CHANS), lambda i, s: (0, i, 0, 0))
    else:
        x_spec = pl.BlockSpec((None, 1, RES, CHANS), lambda i, s: (member, i, 0, 0))
    bias_spec = pl.BlockSpec((DEVS, 1, HEADS * ROWS, RES), lambda i, s: (0, member, 0, 0))
    out_shape = jax.ShapeDtypeStruct((DEVS, ROWS, ROWS, CHANS), BF)
    bias_rows = 16 if flipped else HEADS * ROWS
    bias_shape = jax.ShapeDtypeStruct((bias_rows, RES), BF)
    return pl.pallas_call(
        partial(attend_kernel, flipped),
        grid_spec=pltpu.PrefetchScalarGridSpec(
            num_scalar_prefetch=1,
            grid=(ROWS,),
            in_specs=[x_spec, bias_spec]
            + [whole(a) for a in (gain, shift, gain2, shift2, w, wkt, wo, extra, down)],
            out_specs=[whole(out_shape), whole(bias_shape)],
            scratch_shapes=[
                pltpu.VMEM((HEADS, RES, RES), F32),
                pltpu.VMEM((HEADS, RES, 2 * CHANS), BF),
                pltpu.VMEM((HEADS, RES, CHANS), BF),
                pltpu.VMEM((CHANS, RES), BF),
                pltpu.VMEM((RES, CHANS), F32),
                pltpu.VMEM((RES, CHANS), F32),
                pltpu.VMEM((RES * ROWS, CHANS), F32),
                pltpu.VMEM((HEADS * ROWS, RES), F32),
            ],
        ),
        out_shape=[out_shape, bias_shape],
        compiler_params=pltpu.CompilerParams(vmem_limit_bytes=VMEM_LIMIT),
        cost_estimate=pl.CostEstimate(
            flops=30_000_000_000, bytes_accessed=8_000_000, transcendentals=0
        ),
        name="attend_columns" if flipped else "attend_rows",
    )(info, state, bias, gain, shift, gain2, shift2, w, wkt, wo, extra, down)


def join_kernel(x_ref, out_ref, line):
    for e in range(DEVS):
        line[pl.ds(e, ROWS, stride=DEVS), :] = x_ref[e, 0].astype(F32)
    out_ref[0] = line[...].astype(BF)


def join(state):
    return pl.pallas_call(
        join_kernel,
        grid=(ROWS,),
        in_specs=[pl.BlockSpec((DEVS, 1, ROWS, CHANS), lambda i: (0, i, 0, 0))],
        out_specs=pl.BlockSpec((1, RES, CHANS), lambda i: (i, 0, 0)),
        out_shape=jax.ShapeDtypeStruct((ROWS, RES, CHANS), BF),
        scratch_shapes=[pltpu.VMEM((RES, CHANS), F32)],
        name="join",
    )(state)


def swap_blocks(state):
    return lax.all_to_all(state, "dap", 0, 0, tiled=True)


def on_device(
    pair_state, lengths, norm_gain, norm_shift, attn_proj, bias_proj, attn_out, trans_up, trans_down
):
    group = lax.axis_index("grp")
    me = lax.axis_index("dap")
    pairs = pair_state.shape[0]
    gains = [norm_gain[m : m + 1] for m in range(3)]
    shifts = [norm_shift[m : m + 1] for m in range(3)]
    w_qvg = [
        jnp.concatenate([attn_proj[m, :, :CHANS], attn_proj[m, :, 2 * CHANS :]], 1)
        for m in range(2)
    ]
    w_kt = [attn_proj[m, :, CHANS : 2 * CHANS].T for m in range(2)]
    bpt = [jnp.pad(bias_proj[m].T, ((0, 16 - HEADS), (0, 0))) for m in range(2)]
    lens = [lax.dynamic_index_in_dim(lengths, group * pairs + p, 0, keepdims=False) for p in range(pairs)]
    row_info = [jnp.stack([n, me * ROWS, 1]).astype(jnp.int32) for n in lens]
    col_info = [jnp.stack([n, me, DEVS]).astype(jnp.int32) for n in lens]

    bias0 = lax.all_gather(first_bias(pair_state, gains[0], shifts[0], bpt[0]), "dap", axis=0)
    moved, bias1 = [], []
    for p in range(pairs):
        first, local = attend(
            False, p, row_info[p], pair_state, bias0, gains[0], shifts[0], gains[1], shifts[1],
            w_qvg[0], w_kt[0], attn_out[0], bpt[1], trans_down,
        )
        bias1.append(lax.all_gather(local[None], "dap", axis=0))
        moved.append(swap_blocks(first))
    outs = []
    for p in range(pairs):
        third, _ = attend(
            True, 0, col_info[p], moved[p], bias1[p], gains[1], shifts[1], gains[2], shifts[2],
            w_qvg[1], w_kt[1], attn_out[1], trans_up, trans_down,
        )
        outs.append(join(swap_blocks(third)))
    return jnp.stack(outs)


def solution(mesh):
    in_specs = (P("grp", "dap", None, None), P(), P(), P(), P(), P(), P(), P(), P())
    out_specs = P("grp", "dap", None, None)
    return jax.shard_map(
        on_device, mesh=mesh, in_specs=in_specs, out_specs=out_specs, check_vma=False
    )
```

time: 1210 us -> 471 us (0.39); the launches traced: 1190 us -> 473 us
  Pallas kernels: 0 us -> 322 us
  other arithmetic: 278 us -> 6.84 us
  blocking collectives: 227 us -> 0 us
  local copies, waits for them, and re-layouts: 208 us -> 9.01 us
  matrix products: 175 us -> 0 us
  loops' own time: 97.1 us -> 0 us
  waiting for transfers between devices: 183 us -> 98.9 us
  starting transfers between devices: 6.03 us -> 22.8 us
    pallas_call x0 -> x7, Pallas kernels: none -> 322 us  [the longest x4 279 us: attend(): pl.pallas_call(partial(attend_kernel, flipped), grid_spec=pltpu.PrefetchS...]
    all_to_all x3 -> x0, blocking collectives: 227 us -> none  [the longest x1 117 us: on_device(): lax.all_to_all(homeward, 'grp', split_axis=0, concat_axis=0, tiled=True)]
    dot_general x138 -> x0, matrix products: 175 us -> none  [the longest x48 57.9 us: one_step(): jnp.einsum('rhjk,rkhd->rhjd', weights.astype(jnp.bfloat16), value_part, p...]
    convert_element_type x87 -> x0, other arithmetic: 127 us -> none  [the longest x48 56.2 us: one_step(): scores = scores + bias_part.astype(jnp.float32)[None]]
    reduce_sum x58 -> x0, other arithmetic: 112 us -> none  [the longest x3 51.6 us: layer_norm(): spread = jnp.mean(center * center, -1, keepdims=True)]
    another operation x46 -> x0, loops' own time: 97.1 us -> none  [the longest x24 69.2 us: one_block(): return lax.cond(first_row + start < length, work, skipped, start)]
    all_to_all x1 -> x4, waiting for transfers between devices: 85.6 us -> 18 us  [swap_blocks(): return lax.all_to_all(state, 'dap', 0, 0, tiled=True)]
    dynamic_update_slice x25 -> x0, local copies, waits for them, and re-layouts: 43.6 us -> none  [the longest x24 40.9 us: masked_blocks(): return lax.map(one_block, starts).reshape(rows_dev, width_all, chans)]
  transfers between devices with their start and end apart: 3 -> 7, of which waited for: 3 -> 3; matrix products, arithmetic and copies ran while one was open for 2% -> 1% of each run, Pallas kernels for 0% -> 51%
where the time goes in v1:
time: 471 us; the launch traced here: 473 us
  Pallas kernels  322 us (68%)
  waiting for transfers between devices  98.9 us (21%)
  starting transfers between devices  22.8 us (5%)
  between operations  13.3 us (3%)
  local copies, waits for them, and re-layouts  9.01 us (2%)
  other arithmetic  6.84 us (1%)
    pallas_call x4, Pallas kernels, attend(): pl.pallas_call(partial(attend_kernel, flipped), grid_spec=pltpu.PrefetchS...  279 us
    all_gather x1, waiting for transfers between devices, on_device(): lax.all_gather(first_bias(pair_state, gains[0], shifts[0], bpt[0]), 'dap'...  46.6 us
    all_gather x2, waiting for transfers between devices, on_device(): bias1.append(lax.all_gather(local[None], 'dap', axis=0))  34.3 us
    all_to_all x4, starting transfers between devices, swap_blocks(): return lax.all_to_all(state, 'dap', 0, 0, tiled=True)  22.6 us
    pallas_call x2, Pallas kernels, join(): pl.pallas_call(join_kernel, grid=(ROWS,), in_specs=[pl.BlockSpec((DEVS, 1...  21.7 us
    pallas_call x1, Pallas kernels, first_bias(): pl.pallas_call(first_bias_kernel, grid=(pairs, ROWS), in_specs=[pl.BlockS...  21.5 us
    all_to_all x4, waiting for transfers between devices, swap_blocks(): return lax.all_to_all(state, 'dap', 0, 0, tiled=True)  18 us
  transfers between devices with their start and end apart: 7, of which 3 were waited for; matrix products, arithmetic and copies ran while one was open for 1% of the time, Pallas kernels for 51%

profile of v1, /device:TPU:6, one launch (start us, length us, event | category | flops | bytes accessed | tf_op | source)
XLA Modules:
  0.0 473.0 jit_solution(13095620751581959472)
XLA Ops:
  6.5 0.0 all-gather.7.cloned.1.call-start
  6.5 0.7 slice_bitcast_fusion.6
  7.2 0.6 pad.7.bpt_ref
  7.8 1.4 fusion.1
  9.2 0.0 copy-start.9
  9.2 0.0 copy-start.11
  9.2 0.0 copy-start.10
  9.2 0.0 copy-start.3
  9.2 0.0 copy-start.4
  9.2 0.0 copy-start.5
  9.3 21.5 %first_bias.1 = bf16[2,64,512]{2,1,0:T(8,128)(2,1)} custom-call(bf16[2,16,512,128]{3,2,1,0:T(8,128)(2,1)} %x_ref.5, f32[1,128]{1,0:T(1,128)} %get-tuple-element.38.gain_ref, f32[1,128]{1,0:T(1,128)} %get-tuple-element.26.shift_ref, bf16[16,128]{1,0:T(8,128)(2,1)} %pad.7.bpt_ref), custom_call_target="tpu_custom_call" | custom-call | tf_op jit(solution)/shard_map/first_bias/pallas_call | solution.py:56
  30.8 0.0 all-gather.7.cloned.1.call-update
  30.8 0.0 all-gather.11.cloned.1.call-start
  30.9 0.0 copy-done.9
  30.9 0.1 copy.14
  31.1 0.0 copy-done.11
  31.1 0.7 fusion.3
  31.7 1.4 pad_add_fusion.2
  33.1 0.0 copy-done.10
  33.2 46.6 %all-gather.7.cloned.1.call-done = bf16[64,64,512]{2,1,0:T(8,128)(2,1)} async-done(((bf16[2,64,512]{2,1,0:T(8,128)(2,1)}), bf16[64,64,512]{2,1,0:T(8,128)(2,1)}) %all-gather.7.cloned.1.call-update) | async-done | bytes 4194320 | tf_op jit(solution)/shard_map/all_gather | solution.py:286
  79.7 0.0 copy-done.3
  79.7 0.0 copy-done.4
  79.7 0.0 copy-done.5
  79.7 47.9 %attend_rows.3 = (bf16[32,16,16,128]{3,2,1,0:T(8,128)(2,1)S(1)}, bf16[64,512]{1,0:T(8,128)(2,1)}) custom-call(s32[3]{0:T(128)S(1)} %get-tuple-element.35.info_ref, bf16[2,16,512,128]{3,2,1,0:T(8,128)(2,1)} %x_ref.5, bf16[32,2,64,512]{3,2,1,0:T(8,128)(2,1)} %bitcast.39, f32[1,128]{1,0:T(1,128)S(1)} %copy-done.4, f32[1,128]{1,0:T(1,128)S(1)} %copy-done.3, ...), custom_call_target="tpu_custom_call" | custom-call | flops 30000001024 | bytes 8000000 | tf_op jit(solution)/shard_map/attend_rows/pallas_call | solution.py:218
  127.7 0.0 copy-start.1
  127.7 1.3 copy-done.1
  129.0 0.0 all-gather.11.cloned.1.call-update
  129.0 4.1 all-to-all-start.2
  133.1 0.2 all-gather.9.cloned.1.call-start
  133.3 103.4 %attend_rows.2 = (bf16[32,16,16,128]{3,2,1,0:T(8,128)(2,1)S(1)}, bf16[64,512]{1,0:T(8,128)(2,1)}) custom-call(s32[3]{0:T(128)S(1)} %get-tuple-element.36.info_ref, bf16[2,16,512,128]{3,2,1,0:T(8,128)(2,1)} %x_ref.5, bf16[32,2,64,512]{3,2,1,0:T(8,128)(2,1)} %bitcast.40, f32[1,128]{1,0:T(1,128)S(1)} %copy-done.4, f32[1,128]{1,0:T(1,128)S(1)} %copy-done.3, ...), custom_call_target="tpu_custom_call" | custom-call | flops 30000001024 | bytes 8000000 | tf_op jit(solution)/shard_map/attend_rows/pallas_call | solution.py:218
  236.8 0.0 copy-start
  236.8 1.4 copy-done
  238.2 0.0 all-gather.9.cloned.1.call-update
  238.2 0.1 copy.15
  238.3 0.8 pad_add_fusion.1.info_ref
  239.1 0.7 pad_add_fusion.info_ref
  239.8 0.0 all-to-all-done.2.x_ref
  239.8 0.0 copy-start.6
  239.8 7.9 %all-to-all-start = ((bf16[32,16,16,128]{3,2,1,0:T(8,128)(2,1)}), bf16[32,16,16,128]{3,2,1,0:T(8,128)(2,1)}, u32[]{:S(2)}, u32[]{:S(2)}) async-start(bf16[32,16,16,128]{3,2,1,0:T(8,128)(2,1)} %copy-done), calls=%async_computation | async-start | bytes 4194304 | tf_op jit(solution)/shard_map/all_to_all | solution.py:265
  247.7 0.0 all-gather.11.cloned.1.call-done
  247.7 0.0 copy-done.6
  247.7 29.7 %attend_columns.3 = (bf16[32,16,16,128]{3,2,1,0:T(8,128)(2,1)S(1)}, bf16[16,512]{1,0:T(8,128)(2,1)}) custom-call(s32[3]{0:T(128)S(1)} %pad_add_fusion.info_ref, bf16[32,16,16,128]{3,2,1,0:T(8,128)(2,1)S(1)} %all-to-all-done.2.x_ref, bf16[32,1,64,512]{3,2,1,0:T(8,128)(2,1)} %bitcast.41, f32[1,128]{1,0:T(1,128)S(1)} %get-tuple-element.37.gain2_ref.gain_ref, ...), custom_call_target="tpu_custom_call" | custom-call | flops 30000001024 | bytes 8000000 | tf_op jit(solution)/shard_map/attend_columns/pallas_call | solution.py:218
  277.5 0.0 copy-start.2
  277.5 1.3 copy-done.2
  278.8 0.0 all-to-all-done.x_ref
  278.8 5.8 %all-to-all-start.3 = ((bf16[32,16,16,128]{3,2,1,0:T(8,128)(2,1)}), bf16[32,16,16,128]{3,2,1,0:T(8,128)(2,1)S(1)}, u32[]{:S(2)}, u32[]{:S(2)}) async-start(bf16[32,16,16,128]{3,2,1,0:T(8,128)(2,1)} %copy-done.2), calls=%async_computation.3 | async-start | bytes 4194304 | tf_op jit(solution)/shard_map/all_to_all | solution.py:265
  284.6 34.3 %all-gather.9.cloned.1.call-done = bf16[2048,512]{1,0:T(8,128)(2,1)} async-done(((bf16[64,512]{1,0:T(8,128)(2,1)}), bf16[2048,512]{1,0:T(8,128)(2,1)}) %all-gather.9.cloned.1.call-update) | async-done | bytes 2097168 | tf_op jit(solution)/shard_map/all_gather | solution.py:293
  319.0 97.7 %attend_columns.2 = (bf16[32,16,16,128]{3,2,1,0:T(8,128)(2,1)}, bf16[16,512]{1,0:T(8,128)(2,1)}) custom-call(s32[3]{0:T(128)S(1)} %pad_add_fusion.1.info_ref, bf16[32,16,16,128]{3,2,1,0:T(8,128)(2,1)} %all-to-all-done.x_ref, bf16[32,1,64,512]{3,2,1,0:T(8,128)(2,1)} %bitcast.42, f32[1,128]{1,0:T(1,128)S(1)} %get-tuple-element.37.gain2_ref.gain_ref, ...), custom_call_target="tpu_custom_call" | custom-call | flops 30000001024 | bytes 8000000 | tf_op jit(solution)/shard_map/attend_columns/pallas_call | solution.py:218
  416.7 0.0 all-to-all-done.3.x_ref
  416.7 0.0 copy-start.7
  416.7 1.3 copy-done.7
  418.0 4.8 %all-to-all-start.1 = ((bf16[32,16,16,128]{3,2,1,0:T(8,128)(2,1)}), bf16[32,16,16,128]{3,2,1,0:T(8,128)(2,1)}, u32[]{:S(2)}, u32[]{:S(2)}) async-start(bf16[32,16,16,128]{3,2,1,0:T(8,128)(2,1)} %get-tuple-element.13), calls=%async_computation.1 | async-start | bytes 4194304 | tf_op jit(solution)/shard_map/all_to_all | solution.py:265
  422.8 10.9 %join.3 = bf16[16,512,128]{2,1,0:T(8,128)(2,1)} custom-call(bf16[32,16,16,128]{3,2,1,0:T(8,128)(2,1)} %copy-done.7), custom_call_target="tpu_custom_call" | custom-call | tf_op jit(solution)/shard_map/join/pallas_call | solution.py:253
  433.7 0.0 copy-start.8
  433.7 18.0 %all-to-all-done.1.x_ref = bf16[32,16,16,128]{3,2,1,0:T(8,128)(2,1)} async-done(((bf16[32,16,16,128]{3,2,1,0:T(8,128)(2,1)}), bf16[32,16,16,128]{3,2,1,0:T(8,128)(2,1)}, u32[]{:S(2)}, u32[]{:S(2)}) %all-to-all-start.1) | async-done | bytes 2097184 | tf_op jit(solution)/shard_map/all_to_all | solution.py:265
  451.6 10.8 %join.2 = bf16[16,512,128]{2,1,0:T(8,128)(2,1)} custom-call(bf16[32,16,16,128]{3,2,1,0:T(8,128)(2,1)} %all-to-all-done.1.x_ref), custom_call_target="tpu_custom_call" | custom-call | tf_op jit(solution)/shard_map/join/pallas_call | solution.py:253
  462.5 0.0 copy-done.8
  462.5 4.0 pad_maximum_fusion
  (6 shorter events, 0.1 us)
Async XLA Ops:
  6.5 73.2 %all-gather.7.cloned.1.call-start = ((), (), s32[]{:S(2)}) async-start(), calls=%async_computation.4 | async-start | bytes 4325376 | tf_op jit(solution)/shard_map/all_gather | solution.py:286
  9.2 21.7 %copy-start.9 = (bf16[2,128,512]{2,1,0:T(8,128)(2,1)S(1)}, bf16[2,128,512]{2,1,0:T(8,128)(2,1)}, u32[]{:S(2)}) copy-start(bf16[2,128,512]{2,1,0:T(8,128)(2,1)} %param.13) | copy-start | bytes 786436
  9.2 21.8 %copy-start.11 = (s32[8]{0:T(128)S(1)}, s32[8]{0:T(128)}, u32[]{:S(2)}) copy-start(s32[8]{0:T(128)} %param.10) | copy-start | bytes 100
  9.2 23.9 %copy-start.10 = (bf16[2,128,128]{2,1,0:T(8,128)(2,1)S(1)}, bf16[2,128,128]{2,1,0:T(8,128)(2,1)}, u32[]{:S(2)}) copy-start(bf16[2,128,128]{2,1,0:T(8,128)(2,1)} %param.15) | copy-start | bytes 196612
  9.2 70.5 %copy-start.3 = (f32[1,128]{1,0:T(1,128)S(1)}, f32[1,128]{1,0:T(1,128)}, u32[]{:S(2)}) copy-start(f32[1,128]{1,0:T(1,128)} %get-tuple-element.26.shift_ref) | copy-start | bytes 1540
  9.2 70.5 %copy-start.4 = (f32[1,128]{1,0:T(1,128)S(1)}, f32[1,128]{1,0:T(1,128)}, u32[]{:S(2)}) copy-start(f32[1,128]{1,0:T(1,128)} %get-tuple-element.38.gain_ref) | copy-start | bytes 1540
  9.2 70.5 %copy-start.5 = (bf16[512,128]{1,0:T(8,128)(2,1)S(1)}, bf16[512,128]{1,0:T(8,128)(2,1)}, u32[]{:S(2)}) copy-start(bf16[512,128]{1,0:T(8,128)(2,1)} %down_ref.7) | copy-start | bytes 393220
  30.8 216.9 %all-gather.11.cloned.1.call-start = ((), (), s32[]{:S(2)}) async-start(), calls=%async_computation.6 | async-start | bytes 2162688 | tf_op jit(solution)/shard_map/all_gather | solution.py:293
  127.7 1.3 copy-start.1
  129.0 110.8 %all-to-all-start.2 = ((bf16[32,16,16,128]{3,2,1,0:T(8,128)(2,1)}), bf16[32,16,16,128]{3,2,1,0:T(8,128)(2,1)S(1)}, u32[]{:S(2)}, u32[]{:S(2)}) async-start(bf16[32,16,16,128]{3,2,1,0:T(8,128)(2,1)} %copy-done.1), calls=%async_computation.2 | async-start | bytes 4194304 | tf_op jit(solution)/shard_map/all_to_all | solution.py:265
  133.1 185.9 %all-gather.9.cloned.1.call-start = ((), (), s32[]{:S(2)}) async-start(), calls=%async_computation.5 | async-start | bytes 2162688 | tf_op jit(solution)/shard_map/all_gather | solution.py:293
  236.8 1.4 copy-start
  239.8 7.9 %copy-start.6 = (bf16[128,512]{1,0:T(8,128)(2,1)S(1)}, bf16[128,512]{1,0:T(8,128)(2,1)}, u32[]{:S(2)}) copy-start(bf16[128,512]{1,0:T(8,128)(2,1)} %extra_ref.3) | copy-start | bytes 393220
  239.8 39.0 %all-to-all-start = ((bf16[32,16,16,128]{3,2,1,0:T(8,128)(2,1)}), bf16[32,16,16,128]{3,2,1,0:T(8,128)(2,1)}, u32[]{:S(2)}, u32[]{:S(2)}) async-start(bf16[32,16,16,128]{3,2,1,0:T(8,128)(2,1)} %copy-done), calls=%async_computation | async-start | bytes 4194304 | tf_op jit(solution)/shard_map/all_to_all | solution.py:265
  277.5 1.3 copy-start.2
  278.8 137.9 %all-to-all-start.3 = ((bf16[32,16,16,128]{3,2,1,0:T(8,128)(2,1)}), bf16[32,16,16,128]{3,2,1,0:T(8,128)(2,1)S(1)}, u32[]{:S(2)}, u32[]{:S(2)}) async-start(bf16[32,16,16,128]{3,2,1,0:T(8,128)(2,1)} %copy-done.2), calls=%async_computation.3 | async-start | bytes 4194304 | tf_op jit(solution)/shard_map/all_to_all | solution.py:265
  416.7 1.3 copy-start.7
  418.0 33.6 %all-to-all-start.1 = ((bf16[32,16,16,128]{3,2,1,0:T(8,128)(2,1)}), bf16[32,16,16,128]{3,2,1,0:T(8,128)(2,1)}, u32[]{:S(2)}, u32[]{:S(2)}) async-start(bf16[32,16,16,128]{3,2,1,0:T(8,128)(2,1)} %get-tuple-element.13), calls=%async_computation.1 | async-start | bytes 4194304 | tf_op jit(solution)/shard_map/all_to_all | solution.py:265
  433.7 28.8 %copy-start.8 = (bf16[16,512,128]{2,1,0:T(8,128)(2,1)S(1)}, bf16[16,512,128]{2,1,0:T(8,128)(2,1)}, u32[]{:S(2)}) copy-start(bf16[16,512,128]{2,1,0:T(8,128)(2,1)} %join.3) | copy-start | bytes 6291460
Sparse Core Ops, SparseCore 0:
  30.9 48.7 all-gather.6
  129.1 107.3 all-gather.10
  238.8 80.0 all-gather.8

commit v2 on v1

v2 whole, which is shorter than its diff:
```python
from functools import partial

import jax
import jax.numpy as jnp
from jax import lax
from jax.experimental import pallas as pl
from jax.experimental.pallas import tpu as pltpu
from jax.sharding import PartitionSpec as P

HEADS = 4
HEAD_DIM = 32
CHANS = 128
RES = 512
DEVS = 32
ROWS = 16
HIDDEN = 512
EPSILON = 1e-05
LOG2E = 1.4426950408889634
MASKED = -1e30
PARTS = 1
EXTRA = 8
COLUMN_CUTS = (((0, 16),), ((0, 16),))
DEN_LOW = 2.0**-60
DEN_HIGH = 2.0**60
WIDTHS = (256, 384, 512)
BF = jnp.bfloat16
F32 = jnp.float32
VMEM_LIMIT = 48 * 2**20


def dot_nn(left, right):
    return jnp.dot(left, right, preferred_element_type=F32)


def dot_nt(left, right):
    return lax.dot_general(left, right, (((1,), (1,)), ((), ())), preferred_element_type=F32)


def spread_norm(values, ones, gain_row, shift_row):
    wide = values.astype(F32)
    center = wide - jnp.mean(wide, -1, keepdims=True)
    spread = jnp.mean(center * center, -1, keepdims=True)
    return (center * lax.rsqrt(spread + EPSILON) * gain_row + shift_row).astype(BF)


def mean_matrix():
    return jnp.full((CHANS, CHANS), 1.0 / CHANS, F32).astype(BF)


def first_bias_kernel(x_ref, gain_ref, shift_ref, bpt_ref, out_ref, rows_scr):
    ones = mean_matrix()

    def one_row(r, _):
        y = spread_norm(x_ref[r], ones, gain_ref[...], shift_ref[...])
        b = dot_nt(bpt_ref[...], y)
        for h in range(HEADS):
            rows_scr[pl.ds(h * ROWS + r, 1), :] = b[h : h + 1]
        return 0

    lax.fori_loop(0, ROWS, one_row, 0, unroll=2)
    out_ref[...] = rows_scr[...].astype(BF)


def first_bias(member, state, gain, shift, bpt):
    whole = lambda a: pl.BlockSpec(a.shape, lambda i: (0,) * a.ndim)
    return pl.pallas_call(
        first_bias_kernel,
        grid=(1,),
        in_specs=[pl.BlockSpec((None, ROWS, RES, CHANS), lambda i: (member, 0, 0, 0))]
        + [whole(a) for a in (gain, shift, bpt)],
        out_specs=pl.BlockSpec((HEADS * ROWS, RES), lambda i: (0, 0)),
        out_shape=jax.ShapeDtypeStruct((HEADS * ROWS, RES), BF),
        scratch_shapes=[pltpu.VMEM((HEADS * ROWS, RES), F32)],
        compiler_params=pltpu.CompilerParams(vmem_limit_bytes=VMEM_LIMIT),
        name="first_bias",
    )(state, gain, shift, bpt)


def attend_kernel(
    flipped,
    column,
    count,
    info_ref,
    x_ref,
    bias_ref,
    bias_more_ref,
    gain_ref,
    shift_ref,
    gain2_ref,
    shift2_ref,
    w_ref,
    wkt_ref,
    wo_ref,
    extra_ref,
    down_ref,
    out_ref,
    biasf,
    vblk_a,
    vblk_b,
    qm_a,
    qm_b,
    kts_a,
    kts_b,
    gate_a,
    gate_b,
    gated_a,
    gated_b,
    line,
    bias_rows,
    low_den,
    high_den,
):
    n = info_ref[0]
    first_row = info_ref[1]
    stride = info_ref[2]
    parity = info_ref[3]
    live_rows = jnp.clip((n - first_row + stride - 1) // stride - column, 0, count)
    head_of = lax.broadcasted_iota(jnp.int32, (1, CHANS), 1) // HEAD_DIM
    ones = mean_matrix()
    side_a = (vblk_a, qm_a, kts_a, gate_a)
    side_b = (vblk_b, qm_b, kts_b, gate_b)

    def load_x(r, start, size):
        if flipped:
            return x_ref[start // ROWS : (start + size) // ROWS, column + r].reshape(size, CHANS)
        return x_ref[r, start : start + size]

    def put(r, start, values):
        line[pl.ds(start * count + r, values.shape[0], stride=count), :] = values

    klive = lax.broadcasted_iota(jnp.int32, (1, RES), 1) < n
    def hold(h, at, b):
        b = jnp.where(klive, b.astype(F32) * LOG2E, MASKED)
        biasf[h, at] = b - jnp.max(b, -1, keepdims=True)

    if flipped:
        for ref, base, first_head in (
            (bias_ref, 0, 2 * parity),
            (bias_more_ref, 0, 2 - 2 * parity),
        ):
            for t in range(EXTRA):
                q = t % 4
                b = ref[:, base + t].reshape(RES, CHANS).astype(F32).T
                hold(first_head + t // 4, slice(q * CHANS, (q + 1) * CHANS), b)
    else:

        def place(t, _):
            for ref, base in ((bias_ref, 4), (bias_more_ref, 4 + DEVS // 2)):
                at = pl.ds(pl.multiple_of(info_ref[base + t] * ROWS, ROWS), ROWS)
                for h in range(HEADS):
                    hold(h, at, ref[t, h * ROWS : (h + 1) * ROWS])
            return 0

        lax.fori_loop(0, DEVS // 2, place, 0, unroll=2)
    for h in range(HEADS):
        tail = jnp.broadcast_to((head_of == h).astype(F32).astype(BF), (RES, CHANS))
        vblk_a[h, :, CHANS:] = tail
        vblk_b[h, :, CHANS:] = tail
    low_den[...] = jnp.ones_like(low_den)
    high_den[...] = jnp.ones_like(high_den)

    def prologue(r, side, start, size):
        vblk, qm, kts, gate = side
        at = slice(start, start + size)
        y = spread_norm(load_x(r, start, size), ones, gain_ref[...], shift_ref[...])
        proj = dot_nn(y, w_ref[...])
        q = proj[:, :CHANS] * (HEAD_DIM**-0.5 * LOG2E)
        v = proj[:, CHANS : 2 * CHANS]
        gate[at] = jax.nn.sigmoid(proj[:, 2 * CHANS :])
        kts[:, at] = dot_nt(wkt_ref[...], y).astype(BF)
        for h in range(HEADS):
            qm[h, at] = jnp.where(head_of == h, q, 0.0).astype(BF)
            vblk[h, at, :CHANS] = jnp.where(head_of == h, v, 0.0).astype(BF)

    def one_head(side, h, width):
        vblk, qm, kts, _ = side
        s = dot_nn(qm[h, :width], kts[:, :width]) + biasf[h, :width, :width]
        return dot_nn(jnp.exp2(s).astype(BF), vblk[h, :width])

    def finish_heads(acc, side, gated, width):
        den = acc[:, CHANS:]
        live = lax.broadcasted_iota(jnp.int32, (width, 1), 0) < n
        shown = jnp.where(live, den, 1.0).reshape(width // 8, 8, CHANS)
        low_den[...] = jnp.minimum(low_den[...], jnp.min(shown, 0))
        high_den[...] = jnp.maximum(high_den[...], jnp.max(shown, 0))
        gated[:width] = (acc[:, :CHANS] / den * side[3][:width]).astype(BF)

    def epilogue(r, gated, start, size):
        live = start + lax.broadcasted_iota(jnp.int32, (size, 1), 0) < n
        update = jnp.where(live, dot_nn(gated[start : start + size], wo_ref[...]), 0.0)
        result = (load_x(r, start, size).astype(F32) + update).astype(BF)
        normed = spread_norm(result, ones, gain2_ref[...], shift2_ref[...])
        wide = result.astype(F32)
        if flipped:
            hidden = jax.nn.relu(dot_nn(normed, extra_ref[...])).astype(BF)
            update = jnp.where(live, dot_nn(hidden, down_ref[...]), 0.0)
            put(r, start, wide + update)
        else:
            put(r, start, wide)
            b = dot_nt(extra_ref[...], normed)
            for h in range(HEADS):
                bias_rows[pl.ds(h * ROWS + r, 1), start : start + size] = b[h : h + 1]

    def work(width):
        part = width // PARTS
        chunks = [c * part for c in range(PARTS)]

        def row(r, side, gated):
            for c in chunks:
                prologue(r, side, c, part)
            acc = one_head(side, 0, width)
            for h in range(1, HEADS):
                acc = acc + one_head(side, h, width)
            finish_heads(acc, side, gated, width)
            for c in chunks:
                epilogue(r, gated, c, part)

        def pro(r, side):
            for c in chunks:
                prologue(r, side, c, part)

        def att(side, gated, hook=None):
            acc = one_head(side, 0, width)
            for h in range(1, HEADS):
                if hook is not None:
                    hook(h)
                acc = acc + one_head(side, h, width)
            finish_heads(acc, side, gated, width)

        def epi(r, gated):
            for c in chunks:
                epilogue(r, gated, c, part)

        def pair(u, _):
            ra, rb = 2 * u, 2 * u + 1
            pro(ra, side_a)
            pro(rb, side_b)
            att(side_a, gated_a)
            att(side_b, gated_b)
            epi(ra, gated_a)
            epi(rb, gated_b)
            return 0

        lax.fori_loop(0, live_rows // 2, pair, 0)

        @pl.when(live_rows % 2 == 1)
        def _():
            row(live_rows - 1, side_a, gated_a)

        if width < RES:

            def rest(r, _):
                put(r, width, load_x(r, width, RES - width).astype(F32))
                return 0

            lax.fori_loop(0, live_rows, rest, 0)

        @pl.when(jnp.logical_not((jnp.min(low_den[...]) > DEN_LOW) & (jnp.max(high_den[...]) < DEN_HIGH)))
        def _():
            def careful(r, _):
                for c in chunks:
                    prologue(r, side_a, c, part)

                def block(t, _):
                    at = pl.ds(pl.multiple_of(t * 128, 128), 128)
                    acc = jnp.zeros((128, 2 * CHANS), F32)
                    for h in range(HEADS):
                        s = dot_nn(qm_a[h, at], kts_a[:, :width]) + biasf[h, at, :width]
                        s = s - jnp.max(s, -1, keepdims=True)
                        acc += dot_nn(jnp.exp2(s).astype(BF), vblk_a[h, :width])
                    gated_a[at] = (acc[:, :CHANS] / acc[:, CHANS:] * gate_a[at]).astype(BF)
                    return 0

                lax.fori_loop(0, width // 128, block, 0)
                for c in chunks:
                    epilogue(r, gated_a, c, part)
                return 0

            lax.fori_loop(0, live_rows, careful, 0)

    low = 0
    for width in WIDTHS:

        @pl.when((live_rows > 0) & (n > low) & (n <= width))
        def _(width=width):
            work(width)

        low = width

    def passed(r, _):
        put(r, 0, load_x(r, 0, RES).astype(F32))
        return 0

    lax.fori_loop(live_rows, count, passed, 0)

    def deliver(c, _):
        if flipped:
            size = ROWS * count * 2
            at = pl.ds(pl.multiple_of(c * size, size), size)
            out_ref[pl.ds(2 * c, 2)] = line[at].reshape(2, ROWS, count, CHANS).astype(BF)
        else:
            at = pl.ds(pl.multiple_of(c * RES, RES), RES)
            out_ref[:, c] = line[at].reshape(DEVS, ROWS, CHANS).astype(BF)
        return 0

    lax.fori_loop(0, ROWS, deliver, 0)
    if not flipped:
        for h in range(HEADS):
            for q in range(4):
                piece = bias_rows[h * ROWS : (h + 1) * ROWS, q * CHANS : (q + 1) * CHANS].astype(BF)
                for e in range(h // 2, DEVS, 2):
                    out_ref[e, ROWS + (h % 2) * 4 + q] = piece


def attend(flipped, place, info, state, biases, gain, shift, gain2, shift2, w, wkt, wo, extra, down):
    whole = lambda a: pl.BlockSpec(a.shape, lambda i, s: (0,) * a.ndim)
    if flipped:
        column, count = place
        x_spec = pl.BlockSpec((DEVS, ROWS, ROWS, CHANS), lambda i, s: (0, 0, 0, 0))
        bias_specs = [
            pl.BlockSpec((DEVS, EXTRA, ROWS, CHANS), lambda i, s, at=at: (0, at, 0, 0))
            for _, at in biases
        ]
        out_shape = jax.ShapeDtypeStruct((DEVS, ROWS, count, CHANS), BF)
    else:
        column, count = 0, ROWS
        x_spec = pl.BlockSpec((None, ROWS, RES, CHANS), lambda i, s: (place, 0, 0, 0))
        bias_specs = [
            pl.BlockSpec((DEVS // 2, HEADS * ROWS, RES), lambda i, s, at=at: (at, 0, 0))
            for _, at in biases
        ]
        out_shape = jax.ShapeDtypeStruct((DEVS, ROWS + EXTRA, ROWS, CHANS), BF)
    twice = lambda shape, dtype: [pltpu.VMEM(shape, dtype)] * 2
    return pl.pallas_call(
        partial(attend_kernel, flipped, column, count),
        grid_spec=pltpu.PrefetchScalarGridSpec(
            num_scalar_prefetch=1,
            grid=(1,),
            in_specs=[x_spec]
            + bias_specs
            + [whole(a) for a in (gain, shift, gain2, shift2, w, wkt, wo, extra, down)],
            out_specs=whole(out_shape),
            scratch_shapes=[pltpu.VMEM((HEADS, RES, RES), F32)]
            + twice((HEADS, RES, 2 * CHANS), BF)
            + twice((HEADS, RES, CHANS), BF)
            + twice((CHANS, RES), BF)
            + twice((RES, CHANS), F32)
            + twice((RES, CHANS), BF)
            + [
                pltpu.VMEM((RES * count, CHANS), F32),
                pltpu.VMEM((HEADS * ROWS, RES), F32),
            ]
            + twice((8, CHANS), F32),
        ),
        out_shape=out_shape,
        compiler_params=pltpu.CompilerParams(vmem_limit_bytes=VMEM_LIMIT),
        cost_estimate=pl.CostEstimate(
            flops=30_000_000_000, bytes_accessed=8_000_000, transcendentals=0
        ),
        name="attend_columns" if flipped else "attend_rows",
    )(info, state, biases[0][0], biases[1][0], gain, shift, gain2, shift2, w, wkt, wo, extra, down)


def tail_kernel(x_ref, *refs):
    refs[-1][...] = x_ref[...]


def bias_tail(state, after):
    shape = (DEVS, EXTRA, ROWS, CHANS)
    return pl.pallas_call(
        tail_kernel,
        grid=(1,),
        in_specs=[pl.BlockSpec(shape, lambda i: (0, ROWS // EXTRA, 0, 0))]
        + [pl.BlockSpec(memory_space=pl.ANY)] * len(after),
        out_specs=pl.BlockSpec(shape, lambda i: (0, 0, 0, 0)),
        out_shape=jax.ShapeDtypeStruct(shape, BF),
        name="bias_tail",
    )(state, *after)


def join_kernel(parts, *refs):
    out_ref, line = refs[-2:]

    def one_row(i, _):
        start = 0
        for ref in refs[:parts]:
            size = ref.shape[2]
            for e in range(DEVS):
                line[pl.ds(start * DEVS + e, size, stride=DEVS), :] = ref[e, i].astype(F32)
            start += size
        out_ref[i] = line[...].astype(BF)
        return 0

    lax.fori_loop(0, ROWS, one_row, 0)


def join(member, pieces, earlier):
    more = [] if earlier is None else [earlier]
    return pl.pallas_call(
        partial(join_kernel, len(pieces)),
        grid=(1,),
        in_specs=[pl.BlockSpec(a.shape, lambda i: (0, 0, 0, 0)) for a in pieces]
        + [pl.BlockSpec(memory_space=pl.ANY)] * len(more),
        out_specs=pl.BlockSpec((None, ROWS, RES, CHANS), lambda i: (member, 0, 0, 0)),
        out_shape=jax.ShapeDtypeStruct((2, ROWS, RES, CHANS), BF),
        scratch_shapes=[pltpu.VMEM((RES, CHANS), F32)],
        input_output_aliases={len(pieces): 0} if more else {},
        compiler_params=pltpu.CompilerParams(vmem_limit_bytes=VMEM_LIMIT),
        name="join",
    )(*pieces, *more)


def shifted(state, dy, dz, dc):
    return lax.ppermute(
        state,
        "dap",
        [
            ((y * 4 + z) * 2 + c, ((y + dy) % 4 * 4 + (z + dz) % 4) * 2 + (c ^ dc))
            for y in range(4)
            for z in range(4)
            for c in range(2)
        ],
    )


SHIFTS = (0, 1, -1, 2)


def stack_kernel(*refs):
    out_ref = refs[-1]
    for t in range(len(SHIFTS)):
        out_ref[t] = refs[t][...]


def stack_blocks(blocks, after):
    return pl.pallas_call(
        stack_kernel,
        in_specs=[pl.BlockSpec(memory_space=pltpu.VMEM)] * len(blocks)
        + [pl.BlockSpec(memory_space=pl.ANY)],
        out_specs=pl.BlockSpec(memory_space=pltpu.VMEM),
        out_shape=jax.ShapeDtypeStruct((len(blocks),) + blocks[0].shape, BF),
        name="stack_blocks",
    )(*blocks, after)


def gather_steps(local, after):
    line = stack_blocks([local] + [shifted(local, 0, k, 0) for k in SHIFTS[1:]], after)
    plane = jnp.concatenate([line] + [shifted(line, k, 0, 0) for k in SHIFTS[1:]])
    return plane, shifted(plane, 0, 0, 1)


def gather_order(me):
    y, z, c = me // 8, me // 2 % 4, me % 2
    order = [
        ((y - ky) % 4 * 4 + (z - kz) % 4) * 2 + (c ^ other if other else c)
        for other in range(2)
        for ky in SHIFTS
        for kz in SHIFTS
    ]
    return [jnp.asarray(v, jnp.int32) for v in order]


def swap_blocks(state):
    return lax.all_to_all(state, "dap", 0, 0, tiled=True)


def on_device(
    pair_state, lengths, norm_gain, norm_shift, attn_proj, bias_proj, attn_out, trans_up, trans_down
):
    group = lax.axis_index("grp")
    me = lax.axis_index("dap")
    pairs = pair_state.shape[0]
    gains = [norm_gain[m : m + 1] for m in range(3)]
    shifts = [norm_shift[m : m + 1] for m in range(3)]
    w_qvg = [
        jnp.concatenate([attn_proj[m, :, :CHANS], attn_proj[m, :, 2 * CHANS :]], 1)
        for m in range(2)
    ]
    w_kt = [attn_proj[m, :, CHANS : 2 * CHANS].T for m in range(2)]
    bpt = [jnp.pad(bias_proj[m].T, ((0, 16 - HEADS), (0, 0))) for m in range(2)]
    lens = [lax.dynamic_index_in_dim(lengths, group * pairs + p, 0, keepdims=False) for p in range(pairs)]
    parity = me % 2
    order = [gather_order(me)] + [list(range(DEVS))] * (pairs - 1)
    row_info = [
        jnp.stack([jnp.asarray(v, jnp.int32) for v in [n, me * ROWS, 1, parity] + o])
        for n, o in zip(lens, order)
    ]
    col_info = [jnp.stack([jnp.asarray(v, jnp.int32) for v in [n, me, DEVS, parity]]) for n in lens]

    bias0 = [first_bias(p, pair_state, gains[0], shifts[0], bpt[0]) for p in range(pairs)]
    first_plane, second_plane = gather_steps(bias0[0], bias0[1])
    whole_bias = lax.all_gather(bias0[1], "dap", axis=0)
    biases = [[(first_plane, 0), (second_plane, 0)], [(whole_bias, 0), (whole_bias, 1)]]
    moved = []
    for p in range(pairs):
        first = attend(
            False, p, row_info[p], pair_state, biases[p], gains[0], shifts[0], gains[1], shifts[1],
            w_qvg[0], w_kt[0], attn_out[0], bpt[1], trans_down,
        )
        moved.append(swap_blocks(first))
    result, pieces, third = None, [], None
    for p in range(pairs):
        other = shifted(bias_tail(moved[p], pieces and [third]), 0, 0, 1)
        pieces = []
        for place in COLUMN_CUTS[p]:
            third = attend(
                True, place, col_info[p], moved[p], [(moved[p], 2), (other, 0)], gains[1], shifts[1],
                gains[2], shifts[2], w_qvg[1], w_kt[1], attn_out[1], trans_up, trans_down,
            )
            pieces.append(swap_blocks(third))
        result = join(p, pieces, result)
    return result


def solution(mesh):
    in_specs = (P("grp", "dap", None, None), P(), P(), P(), P(), P(), P(), P(), P())
    out_specs = P("grp", "dap", None, None)
    return jax.shard_map(
        on_device, mesh=mesh, in_specs=in_specs, out_specs=out_specs, check_vma=False
    )
```

time: 471 us -> 552 us (1.17)
  the two profiles are of different devices: /device:TPU:6 before, /device:TPU:1 now
where the time goes in v2:
time: 552 us; the launch traced here: 546 us
  Pallas kernels  409 us (74%)
  waiting for transfers between devices  73.5 us (13%)
  starting transfers between devices  35 us (6%)
  between operations  14.1 us (3%)
  local copies, waits for them, and re-layouts  11.7 us (2%)
    pallas_call x4, Pallas kernels, attend(): pl.pallas_call(partial(attend_kernel, flipped, column, count), grid_spec=...  384 us
    all_to_all x4, waiting for transfers between devices, swap_blocks(): return lax.all_to_all(state, 'dap', 0, 0, tiled=True)  62.3 us
    all_to_all x4, starting transfers between devices, swap_blocks(): return lax.all_to_all(state, 'dap', 0, 0, tiled=True)  22.4 us
    ppermute x9, starting transfers between devices, shifted(): lax.ppermute(state, 'dap', [((y * 4 + z) * 2 + c, ((y + dy) % 4 * 4 + (z...  12.6 us
    pallas_call x2, Pallas kernels, join(): pl.pallas_call(partial(join_kernel, len(pieces)), grid=(1,), in_specs=[pl...  11.8 us
    ppermute x9, waiting for transfers between devices, shifted(): lax.ppermute(state, 'dap', [((y * 4 + z) * 2 + c, ((y + dy) % 4 * 4 + (z...  11.1 us
  transfers between devices with their start and end apart: 14, of which 5 were waited for; matrix products, arithmetic and copies ran while one was open for 1% of the time, Pallas kernels for 72%

profile of v2, /device:TPU:1, one launch (start us, length us, event | category | flops | bytes accessed | tf_op | source)
XLA Modules:
  0.0 546.1 jit_solution(9652065182117352103)
XLA Ops:
  6.5 0.0 all-gather.3.cloned.1.call-start
  6.5 0.7 slice_bitcast_fusion.6
  7.2 0.9 fusion.3
  8.1 2.2 copy-done
  10.3 3.9 first_bias.3.refs_0_
  14.2 0.0 copy-start.8
  14.2 0.0 copy-start.13
  14.2 0.0 copy-start.12
  14.2 4.5 collective-permute-start.2
  18.7 0.4 collective-permute-start.1
  19.1 1.0 collective-permute-start
  20.2 3.9 first_bias.2.refs_4_
  24.0 0.0 copy-start.2
  24.0 0.6 copy-done.2
  24.6 0.0 collective-permute-done.2.refs_3_
  24.7 0.0 collective-permute-done.1.refs_2_
  24.7 0.0 collective-permute-done.refs_1_
  24.7 0.6 copy-done.9
  25.3 0.0 copy-done.10
  25.3 0.6 copy-done.11
  25.9 1.7 stack_blocks.1
  27.6 2.9 collective-permute-start.5
  30.5 0.8 collective-permute-start.4
  31.3 0.7 collective-permute-start.3
  31.9 3.6 collective-permute-done.5
  35.6 7.0 %collective-permute-done.4 = bf16[4,64,512]{2,1,0:T(8,128)(2,1)S(1)} collective-permute-done((bf16[4,64,512]{2,1,0:T(8,128)(2,1)}, bf16[4,64,512]{2,1,0:T(8,128)(2,1)S(1)}, u32[]{:S(2)}, u32[]{:S(2)}) %collective-permute-start.4) | collective-permute-done | bytes 262176 | tf_op jit(solution)/shard_map/ppermute | solution.py:414
  42.6 0.0 collective-permute-done.3
  42.6 1.1 pad_maximum_fusion.bias_ref
  43.6 1.5 collective-permute-start.6
  45.2 0.0 all-gather.3.cloned.1.call-update
  45.5 0.1 copy.13
  45.6 0.0 copy-done.13
  45.6 0.6 fusion.5
  46.2 0.7 stack.164.info_ref
  46.9 0.0 copy-done.12
  46.9 0.5 collective-permute-done.6.bias_more_ref
  47.5 112.0 %attend_rows.3 = bf16[32,24,16,128]{3,2,1,0:T(8,128)(2,1)} custom-call(s32[36]{0:T(128)S(1)} %stack.164.info_ref, bf16[2,16,512,128]{3,2,1,0:T(8,128)(2,1)} %x_ref.7, bf16[16,64,512]{2,1,0:T(8,128)(2,1)S(1)} %pad_maximum_fusion.bias_ref, bf16[16,64,512]{2,1,0:T(8,128)(2,1)S(1)} %collective-permute-done.6.bias_more_ref, ...), custom_call_target="tpu_custom_call" | custom-call | flops 30000001024 | bytes 8000000 | tf_op jit(solution)/shard_map/attend_rows/pallas_call | solution.py:334
  159.4 6.0 %all-to-all-start.1 = ((bf16[32,24,16,128]{3,2,1,0:T(8,128)(2,1)}), bf16[32,24,16,128]{3,2,1,0:T(8,128)(2,1)}, u32[]{:S(2)}, u32[]{:S(2)}) async-start(bf16[32,24,16,128]{3,2,1,0:T(8,128)(2,1)} %attend_rows.3), calls=%async_computation.1 | async-start | bytes 6291456 | tf_op jit(solution)/shard_map/all_to_all | solution.py:464
  165.5 0.7 stack.130.info_ref
  166.1 39.1 %all-to-all-done.1.x_ref.bias_ref = bf16[32,24,16,128]{3,2,1,0:T(8,128)(2,1)} async-done(((bf16[32,24,16,128]{3,2,1,0:T(8,128)(2,1)}), bf16[32,24,16,128]{3,2,1,0:T(8,128)(2,1)}, u32[]{:S(2)}, u32[]{:S(2)}) %all-to-all-start.1) | async-done | bytes 3145760 | tf_op jit(solution)/shard_map/all_to_all | solution.py:464
  205.3 2.3 bias_tail.2
  207.5 0.4 collective-permute-start.7
  208.0 1.6 copy-done.4
  209.5 87.9 %attend_rows.2 = bf16[32,24,16,128]{3,2,1,0:T(8,128)(2,1)} custom-call(s32[36]{0:T(128)S(1)} %stack.130.info_ref, bf16[2,16,512,128]{3,2,1,0:T(8,128)(2,1)} %x_ref.7, bf16[32,64,512]{2,1,0:T(8,128)(2,1)S(1)} %bitcast.66, bf16[32,64,512]{2,1,0:T(8,128)(2,1)S(1)} %bitcast.67, f32[1,128]{1,0:T(1,128)S(1)} %get-tuple-element.24.gain_ref, ...), custom_call_target="tpu_custom_call" | custom-call | flops 30000001024 | bytes 8000000 | tf_op jit(solution)/shard_map/attend_rows/pallas_call | solution.py:334
  297.5 4.8 all-to-all-start
  302.2 0.1 copy.14
  302.4 0.6 fusion.1.info_ref
  303.0 0.0 collective-permute-done.7.bias_more_ref
  303.0 114.1 %attend_columns.2.refs_0_ = bf16[32,16,16,128]{3,2,1,0:T(8,128)(2,1)} custom-call(s32[4]{0:T(128)S(1)} %fusion.1.info_ref, bf16[32,24,16,128]{3,2,1,0:T(8,128)(2,1)} %all-to-all-done.1.x_ref.bias_ref, bf16[32,24,16,128]{3,2,1,0:T(8,128)(2,1)} %all-to-all-done.1.x_ref.bias_ref, bf16[32,8,16,128]{3,2,1,0:T(8,128)(2,1)S(1)} %collective-permute-done.7.bias_more_ref, ...), custom_call_target="tpu_custom_call" | custom-call | flops 30000001024 | bytes 8000000 | tf_op jit(solution)/shard_map/attend_columns/pallas_call | solution.py:334
  417.1 0.0 all-to-all-done.x_ref.bias_ref
  417.1 2.3 bias_tail.3
  419.4 0.3 collective-permute-start.8
  419.7 0.6 fusion.info_ref
  420.3 5.7 %all-to-all-start.3 = ((bf16[32,16,16,128]{3,2,1,0:T(8,128)(2,1)}), bf16[32,16,16,128]{3,2,1,0:T(8,128)(2,1)S(1)}, u32[]{:S(2)}, u32[]{:S(2)}) async-start(bf16[32,16,16,128]{3,2,1,0:T(8,128)(2,1)} %attend_columns.2.refs_0_), calls=%async_computation.3 | async-start | bytes 4194304 | tf_op jit(solution)/shard_map/all_to_all | solution.py:464
  426.0 0.0 collective-permute-done.8.bias_more_ref
  426.0 0.0 copy-start.7
  426.0 0.9 copy-done.7
  426.9 69.8 %attend_columns.3 = bf16[32,16,16,128]{3,2,1,0:T(8,128)(2,1)S(1)} custom-call(s32[4]{0:T(128)S(1)} %fusion.info_ref, bf16[32,24,16,128]{3,2,1,0:T(8,128)(2,1)} %all-to-all-done.x_ref.bias_ref, bf16[32,24,16,128]{3,2,1,0:T(8,128)(2,1)} %all-to-all-done.x_ref.bias_ref, bf16[32,8,16,128]{3,2,1,0:T(8,128)(2,1)S(1)} %collective-permute-done.8.bias_more_ref, ...), custom_call_target="tpu_custom_call" | custom-call | flops 30000001024 | bytes 8000000 | tf_op jit(solution)/shard_map/attend_columns/pallas_call | solution.py:334
  496.7 1.4 copy-done.1
  498.1 0.0 all-to-all-done.3.refs_0_
  498.1 5.9 %all-to-all-start.2 = ((bf16[32,16,16,128]{3,2,1,0:T(8,128)(2,1)}), bf16[32,16,16,128]{3,2,1,0:T(8,128)(2,1)}, u32[]{:S(2)}, u32[]{:S(2)}) async-start(bf16[32,16,16,128]{3,2,1,0:T(8,128)(2,1)} %copy-done.1), calls=%async_computation.2 | async-start | bytes 4194304 | tf_op jit(solution)/shard_map/all_to_all | solution.py:464
  504.0 5.1 join.2.refs_1_
  509.1 23.2 %all-to-all-done.2.refs_0_ = bf16[32,16,16,128]{3,2,1,0:T(8,128)(2,1)} async-done(((bf16[32,16,16,128]{3,2,1,0:T(8,128)(2,1)}), bf16[32,16,16,128]{3,2,1,0:T(8,128)(2,1)}, u32[]{:S(2)}, u32[]{:S(2)}) %all-to-all-start.2) | async-done | bytes 2097184 | tf_op jit(solution)/shard_map/all_to_all | solution.py:464
  532.4 6.7 %join.3 = bf16[2,16,512,128]{3,2,1,0:T(8,128)(2,1)} custom-call(bf16[32,16,16,128]{3,2,1,0:T(8,128)(2,1)} %all-to-all-done.2.refs_0_, bf16[2,16,512,128]{3,2,1,0:T(8,128)(2,1)} %join.2.refs_1_), custom_call_target="tpu_custom_call", output_to_operand_aliasing={{}: (1, {})} | custom-call | tf_op jit(solution)/shard_map/join/pallas_call | solution.py:399
  (21 shorter events, 0.1 us)
Async XLA Ops:
  6.5 201.4 %all-gather.3.cloned.1.call-start = ((), (), s32[]{:S(2)}) async-start(), calls=%async_computation.4 | async-start | bytes 2162688 | tf_op jit(solution)/shard_map/all_gather | solution.py:492
  8.1 2.2 copy-start
  14.1 10.5 %copy-start.3 = (bf16[64,512]{1,0:T(8,128)(2,1)}, bf16[64,512]{1,0:T(8,128)(2,1)S(1)}, u32[]{:S(2)}) copy-start(bf16[64,512]{1,0:T(8,128)(2,1)S(1)} %first_bias.3.refs_0_) | copy-start | bytes 196612
  14.2 31.3 %copy-start.8 = (bf16[2,128,512]{2,1,0:T(8,128)(2,1)S(1)}, bf16[2,128,512]{2,1,0:T(8,128)(2,1)}, u32[]{:S(2)}) copy-start(bf16[2,128,512]{2,1,0:T(8,128)(2,1)} %param.13) | copy-start | bytes 786436
  14.2 31.4 %copy-start.13 = (s32[8]{0:T(128)S(1)}, s32[8]{0:T(128)}, u32[]{:S(2)}) copy-start(s32[8]{0:T(128)} %param.10) | copy-start | bytes 100
  14.2 32.7 %copy-start.12 = (bf16[2,128,128]{2,1,0:T(8,128)(2,1)S(1)}, bf16[2,128,128]{2,1,0:T(8,128)(2,1)}, u32[]{:S(2)}) copy-start(bf16[2,128,128]{2,1,0:T(8,128)(2,1)} %param.15) | copy-start | bytes 196612
  14.2 10.5 %collective-permute-start.2 = (bf16[64,512]{1,0:T(8,128)(2,1)S(1)}, bf16[64,512]{1,0:T(8,128)(2,1)S(1)}, u32[]{:S(2)}, u32[]{:S(2)}) collective-permute-start(bf16[64,512]{1,0:T(8,128)(2,1)S(1)} %first_bias.3.refs_0_), channel_id=1, source_target_pairs={{0,4},{1,5},{2,6},{3,7},{4,0},{5,1},{6,2},{7,3},{8,12},{9,13},{10,... | collective-permute-start | bytes 196616 | tf_op jit(solution)/shard_map/ppermute | solution.py:414
  18.7 6.0 %collective-permute-start.1 = (bf16[64,512]{1,0:T(8,128)(2,1)S(1)}, bf16[64,512]{1,0:T(8,128)(2,1)S(1)}, u32[]{:S(2)}, u32[]{:S(2)}) collective-permute-start(bf16[64,512]{1,0:T(8,128)(2,1)S(1)} %first_bias.3.refs_0_), channel_id=1, source_target_pairs={{0,6},{1,7},{2,0},{3,1},{4,2},{5,3},{6,4},{7,5},{8,14},{9,15},{10,... | collective-permute-start | bytes 196616 | tf_op jit(solution)/shard_map/ppermute | solution.py:414
  19.1 5.5 %collective-permute-start = (bf16[64,512]{1,0:T(8,128)(2,1)S(1)}, bf16[64,512]{1,0:T(8,128)(2,1)S(1)}, u32[]{:S(2)}, u32[]{:S(2)}) collective-permute-start(bf16[64,512]{1,0:T(8,128)(2,1)S(1)} %first_bias.3.refs_0_), channel_id=1, source_target_pairs={{0,2},{1,3},{2,4},{3,5},{4,6},{5,7},{6,0},{7,1},{8,10},{9,11},{10,... | collective-permute-start | bytes 196616 | tf_op jit(solution)/shard_map/ppermute | solution.py:414
  24.0 0.6 copy-start.2
  24.6 22.8 %copy-start.5 = (bf16[512,128]{1,0:T(8,128)(2,1)S(1)}, bf16[512,128]{1,0:T(8,128)(2,1)}, u32[]{:S(2)}) copy-start(bf16[512,128]{1,0:T(8,128)(2,1)} %down_ref.7) | copy-start | bytes 393220
  24.6 0.6 copy-start.9
  24.7 0.6 copy-start.10
  25.3 0.6 copy-start.11
  27.6 8.0 %collective-permute-start.5 = (bf16[4,64,512]{2,1,0:T(8,128)(2,1)}, bf16[4,64,512]{2,1,0:T(8,128)(2,1)S(1)}, u32[]{:S(2)}, u32[]{:S(2)}) collective-permute-start(bf16[4,64,512]{2,1,0:T(8,128)(2,1)} %stack_blocks.1), channel_id=1, source_target_pairs={{0,16},{1,17},{2,18},{3,19},{4,20},{5,21},{6,22},{7,23},{8,24},{9,... | collective-permute-start | bytes 786440 | tf_op jit(solution)/shard_map/ppermute | solution.py:414
  30.5 12.1 %collective-permute-start.4 = (bf16[4,64,512]{2,1,0:T(8,128)(2,1)}, bf16[4,64,512]{2,1,0:T(8,128)(2,1)S(1)}, u32[]{:S(2)}, u32[]{:S(2)}) collective-permute-start(bf16[4,64,512]{2,1,0:T(8,128)(2,1)} %stack_blocks.1), channel_id=1, source_target_pairs={{0,24},{1,25},{2,26},{3,27},{4,28},{5,29},{6,30},{7,31},{8,0},{9,1... | collective-permute-start | bytes 786440 | tf_op jit(solution)/shard_map/ppermute | solution.py:414
  31.3 11.3 %collective-permute-start.3 = (bf16[4,64,512]{2,1,0:T(8,128)(2,1)}, bf16[4,64,512]{2,1,0:T(8,128)(2,1)S(1)}, u32[]{:S(2)}, u32[]{:S(2)}) collective-permute-start(bf16[4,64,512]{2,1,0:T(8,128)(2,1)} %stack_blocks.1), channel_id=1, source_target_pairs={{0,8},{1,9},{2,10},{3,11},{4,12},{5,13},{6,14},{7,15},{8,16},{9,17... | collective-permute-start | bytes 786440 | tf_op jit(solution)/shard_map/ppermute | solution.py:414
  43.6 3.8 collective-permute-start.6
  159.4 45.8 %all-to-all-start.1 = ((bf16[32,24,16,128]{3,2,1,0:T(8,128)(2,1)}), bf16[32,24,16,128]{3,2,1,0:T(8,128)(2,1)}, u32[]{:S(2)}, u32[]{:S(2)}) async-start(bf16[32,24,16,128]{3,2,1,0:T(8,128)(2,1)} %attend_rows.3), calls=%async_computation.1 | async-start | bytes 6291456 | tf_op jit(solution)/shard_map/all_to_all | solution.py:464
  207.5 95.5 %collective-permute-start.7 = (bf16[32,8,16,128]{3,2,1,0:T(8,128)(2,1)}, bf16[32,8,16,128]{3,2,1,0:T(8,128)(2,1)S(1)}, u32[]{:S(2)}, u32[]{:S(2)}) collective-permute-start(bf16[32,8,16,128]{3,2,1,0:T(8,128)(2,1)} %bias_tail.2), channel_id=1, source_target_pairs={{0,1},{1,0},{2,3},{3,2},{4,5},{5,4},{6,7},{7,6},{8,9},{9,8},{10,11... | collective-permute-start | bytes 3145736 | tf_op jit(solution)/shard_map/ppermute | solution.py:414
  208.0 1.6 copy-start.4
  297.5 5.5 %copy-start.6 = (bf16[128,512]{1,0:T(8,128)(2,1)S(1)}, bf16[128,512]{1,0:T(8,128)(2,1)}, u32[]{:S(2)}) copy-start(bf16[128,512]{1,0:T(8,128)(2,1)} %extra_ref.3) | copy-start | bytes 393220
  297.5 119.6 %all-to-all-start = ((bf16[32,24,16,128]{3,2,1,0:T(8,128)(2,1)}), bf16[32,24,16,128]{3,2,1,0:T(8,128)(2,1)}, u32[]{:S(2)}, u32[]{:S(2)}) async-start(bf16[32,24,16,128]{3,2,1,0:T(8,128)(2,1)} %attend_rows.2), calls=%async_computation | async-start | bytes 6291456 | tf_op jit(solution)/shard_map/all_to_all | solution.py:464
  419.4 6.7 %collective-permute-start.8 = (bf16[32,8,16,128]{3,2,1,0:T(8,128)(2,1)}, bf16[32,8,16,128]{3,2,1,0:T(8,128)(2,1)S(1)}, u32[]{:S(2)}, u32[]{:S(2)}) collective-permute-start(bf16[32,8,16,128]{3,2,1,0:T(8,128)(2,1)} %bias_tail.3), channel_id=1, source_target_pairs={{0,1},{1,0},{2,3},{3,2},{4,5},{5,4},{6,7},{7,6},{8,9},{9,8},{10,11... | collective-permute-start | bytes 3145736 | tf_op jit(solution)/shard_map/ppermute | solution.py:414
  420.3 77.8 %all-to-all-start.3 = ((bf16[32,16,16,128]{3,2,1,0:T(8,128)(2,1)}), bf16[32,16,16,128]{3,2,1,0:T(8,128)(2,1)S(1)}, u32[]{:S(2)}, u32[]{:S(2)}) async-start(bf16[32,16,16,128]{3,2,1,0:T(8,128)(2,1)} %attend_columns.2.refs_0_), calls=%async_computation.3 | async-start | bytes 4194304 | tf_op jit(solution)/shard_map/all_to_all | solution.py:464
  426.0 0.9 copy-start.7
  496.7 1.4 copy-start.1
  498.1 34.3 %all-to-all-start.2 = ((bf16[32,16,16,128]{3,2,1,0:T(8,128)(2,1)}), bf16[32,16,16,128]{3,2,1,0:T(8,128)(2,1)}, u32[]{:S(2)}, u32[]{:S(2)}) async-start(bf16[32,16,16,128]{3,2,1,0:T(8,128)(2,1)} %copy-done.1), calls=%async_computation.2 | async-start | bytes 4194304 | tf_op jit(solution)/shard_map/all_to_all | solution.py:464
Sparse Core Ops, SparseCore 0:
  45.3 43.9 all-gather.2
